TPU v7x, 256 devices: a whole 4x4x8 slice. The times are simulated.
256 devices in a mesh: span: 4 (over y), clip: 32 (over x, z), mp: 2 (over core).
Axes of the slice: x: 4, y: 4, z: 8, core: 2. Of those that a mesh axis runs over, the one named last changes fastest.
Arguments:
- queries: bfloat16 [32, 4, 512, 2560], P('clip', 'span', None, 'mp'), may hold values from -8 to 8
- keys: bfloat16 [32, 4, 512, 2560], P('clip', 'span', None, 'mp'), may hold values from -8 to 8
- values: bfloat16 [32, 4, 512, 2560], P('clip', 'span', None, 'mp'), may hold values from -6 to 6
- resid: bfloat16 [32, 4, 512, 5120], P('clip', 'span', None, 'mp'), may hold values from -4 to 4
- out_weight: bfloat16 [2560, 5120], P('clip', 'mp'), may hold values from -0.125 to 0.125
- gate_table: float32 [4, 5120], P(None, 'mp'), may hold values from 4 to 16
- step_scale: float32 [4], replicated, may hold values from 0.5 to 2
- gain: float32 [5120], P('mp'), may hold values from 0.5 to 1.5
- route: int32 [32, 4, 32, 1], P('clip', 'span'), may hold values from 0 to 31; in each aligned block of 32 rows (0 to 31, 32 to 63, ..., all dimensions but the last counted through in order) at most 2 rows name the same one
- clip_len: int32 [32], replicated, may hold values from 1 to 4
- tstep: int32 [32, 4], replicated, may hold values from 0 to 3
Outputs:
- scored: bfloat16 [4, 32, 32, 2, 16, 5120], P('span', 'clip', None, None, None, 'mp')
Inputs may be any that keep to these rules, and one draw needn't show every extreme that they name: `route`: of the 32 blocks of one span, at most 2 go to one group, and some span sends exactly 2 to one group.
All inputs are finite; a program needn't handle non-finite values.
Results may differ from a plain program's by a relative error of at most 0.008.
Values may be sent and summed in bfloat16 or wider, within the bound.
A program may use at most 128 MiB of HBM per device.

v0:
```python
import math

import jax
import jax.numpy as jnp
from jax import lax
from jax.sharding import PartitionSpec as P

HS = 128


def shards(
    queries, keys, values, resid, out_weight, gate_table, step_scale, gain, route, clip_len, tstep
):
    n_span = lax.axis_size("span")
    n_clip = lax.axis_size("clip")
    span_here = lax.axis_index("span")
    clip_here = lax.axis_index("clip")
    tokc = queries.shape[2]
    width = queries.shape[3]
    heads = width // HS
    half = resid.shape[3]
    inv = 1.0 / math.sqrt(HS)
    query = queries[0, 0].reshape(tokc, heads, HS)

    def absorb(carry, key_blk, val_blk, span_id):
        top, total, acc = carry
        key_heads = key_blk.reshape(tokc, heads, HS)
        val_heads = val_blk.reshape(tokc, heads, HS)
        scores = (
            jnp.einsum("qhd,khd->hqk", query, key_heads, preferred_element_type=jnp.float32) * inv
        )
        visible = (span_id >= 0) & (span_id <= span_here)
        scores = jnp.where(visible, scores, -1e30)
        new_top = jnp.maximum(top, jnp.max(scores, axis=-1))
        factor = jnp.exp(top - new_top)
        prob = jnp.exp(scores - new_top[:, :, None])
        total = total * factor + jnp.sum(prob, axis=-1)
        acc = acc * factor[:, :, None] + jnp.einsum(
            "hqk,khd->hqd", prob.astype(jnp.bfloat16), val_heads, preferred_element_type=jnp.float32
        )
        return (new_top, total, acc)

    start_carry = (
        jnp.full((heads, tokc), -1e30, jnp.float32),
        jnp.zeros((heads, tokc), jnp.float32),
        jnp.zeros((heads, tokc, HS), jnp.float32),
    )
    carry = start_carry
    key_piece = lax.all_gather(keys, "span", axis=1, tiled=True)
    val_piece = lax.all_gather(values, "span", axis=1, tiled=True)
    count = key_piece.shape[1]

    def step_one(inner, items):
        key_blk, val_blk, offset = items
        return (absorb(inner, key_blk, val_blk, offset), None)

    carry, unused = lax.scan(
        step_one, carry, (key_piece[0], val_piece[0], jnp.arange(count, dtype=jnp.int32))
    )
    top, total, acc = carry
    attn = (acc / total[:, :, None]).astype(jnp.bfloat16)
    attn = jnp.transpose(attn, (1, 0, 2)).reshape(tokc, width)
    features = lax.all_gather(attn, "mp", axis=1, tiled=True)
    proj = jnp.dot(
        features,
        lax.all_gather(out_weight, "clip", axis=0, tiled=True),
        preferred_element_type=jnp.float32,
    )
    clip_ids = jnp.arange(n_clip, dtype=jnp.int32)
    span_ids = jnp.arange(n_span, dtype=jnp.int32)
    levels = jnp.arange(gate_table.shape[0], dtype=jnp.int32)
    span_pick = (span_ids == span_here).astype(jnp.int32)
    step_src = jnp.sum(tstep * span_pick[None, :], axis=1)
    step_here = jnp.sum(step_src * (clip_ids == clip_here).astype(jnp.int32))
    gate_row = jnp.sum(jnp.where((levels == step_here)[:, None], gate_table, 0.0), axis=0)
    row = (resid[0, 0].astype(jnp.float32) + gate_row[None, :] * proj).astype(jnp.bfloat16)
    row = lax.optimization_barrier(row)
    nblk = route.shape[2]
    brows = tokc // nblk
    slots = max(2, 2 * nblk // n_clip)
    blocks = row.reshape(nblk, brows * half)
    dest = route[0, 0, :, 0]
    onehot = (dest[:, None] == clip_ids[None, :]).astype(jnp.int32)
    before = jnp.cumsum(onehot, axis=0) - onehot
    rank = jnp.sum(before * onehot, axis=1)
    slot_of = dest * slots + rank
    select = (jnp.arange(n_clip * slots, dtype=jnp.int32)[:, None] == slot_of[None, :]).astype(
        jnp.bfloat16
    )
    buffer = jnp.dot(select, blocks, preferred_element_type=jnp.float32).astype(jnp.bfloat16)
    buffer = buffer.reshape(n_clip, slots, brows, half)
    live_src = jnp.where(span_here < clip_len, 1.0, 0.0).astype(jnp.float32)
    scale_src = jnp.sum(
        jnp.where(levels[None, :] == step_src[:, None], step_scale[None, :], 0.0), axis=1
    )
    factor_src = scale_src * live_src
    scored = (
        lax.all_to_all(buffer, "clip", split_axis=0, concat_axis=0, tiled=True).astype(jnp.float32)
        * factor_src[:, None, None, None]
        * gain[None, None, None, :]
    ).astype(jnp.bfloat16)
    return scored[None, None]


def solution(mesh):
    placed = (
        P("clip", "span", None, "mp"),
        P("clip", "span", None, "mp"),
        P("clip", "span", None, "mp"),
        P("clip", "span", None, "mp"),
        P("clip", "mp"),
        P(None, "mp"),
        P(),
        P("mp"),
        P("clip", "span", None, None),
        P(),
        P(),
    )
    return jax.shard_map(
        shards,
        mesh=mesh,
        in_specs=placed,
        out_specs=P("span", "clip", None, None, None, "mp"),
        check_vma=False,
    )
```

profile of v0, /device:TPU:25, one launch (start us, length us, event | category | flops | bytes accessed | tf_op | source)
XLA Modules:
  0.0 546.4 jit_solution(5077960828049887810)
XLA Ops:
  6.5 0.7 all-gather.5.cloned.1.call-update
  7.3 0.7 all-gather.7.cloned.1.call-update
  8.1 0.7 copy.35
  8.8 1.5 copy.38
  10.2 59.3 %all-gather.5.cloned.1.call-done = bf16[1,4,512,1280]{3,2,0,1:T(8,128)(2,1)} async-done(((bf16[1,1,512,1280]{3,2,0,1:T(8,128)(2,1)}), bf16[1,4,512,1280]{3,2,0,1:T(8,128)(2,1)}) %all-gather.5.cloned.1.call-update) | async-done | bytes 5242896 | tf_op jit(solution)/shard_map/all_gather | solution.py:49
  69.6 61.9 %all-gather.7.cloned.1.call-done = bf16[1,4,512,1280]{3,2,0,1:T(8,128)(2,1)} async-done(((bf16[1,1,512,1280]{3,2,0,1:T(8,128)(2,1)}), bf16[1,4,512,1280]{3,2,0,1:T(8,128)(2,1)}) %all-gather.7.cloned.1.call-update) | async-done | bytes 5242896 | tf_op jit(solution)/shard_map/all_gather | solution.py:50
  131.5 109.8 %while.15 = (s32[]{:T(128)}, f32[10,512]{1,0:T(8,128)S(1)}, f32[10,512]{1,0:T(8,128)S(1)}, f32[10,512,128]{2,1,0:T(8,128)}, s32[4]{0:T(128)S(1)}, /*index=5*/s32...) while((s32[]{:T(128)}, f32[10,512]{1,0:T(8,128)S(1)}, ...), condition=%wide.region_8.9_spmd.clone, body=%wide.region_5.8_spmd.clone.sunk | while | flops 1373004800 | bytes 51445920 | solution.py:57
  131.5 0.6 dynamic_slice.19
  133.3 3.0 constant_dynamic-slice_fusion.3
  136.3 1.6 copy.49
  137.9 7.0 %bitcast_reduce_fusion.2 = (f32[10,512]{1,0:T(8,128)S(1)}, f32[10,512,512]{2,1,0:T(8,128)}) fusion(pred[]{:T(512)S(6)} %and.7, bf16[512,10,128]{0,2,1:T(8,128)(2,1)S(1)} %bitcast.57, bf16[512,10,128]{2,0,1:T(8,128)(2,1)} %get-tuple-element.232), kind=kOutput, calls=%fused_computation.1.clone.1 | convolution fusion | flops 678947840 | bytes 13127681 | tf_op jit(solution)/shard_map/while/body/eval_jaxpr/qhd,khd->hqk/dot_general | solution.py:30
  144.9 6.0 %fusion.38 = f32[10,512]{1,0:T(8,128)S(1)} fusion(f32[10,512,512]{2,1,0:T(8,128)} %get-tuple-element.199, f32[10,512]{1,0:T(8,128)S(1)} %select_maximum_fusion.2, pred[]{:T(512)S(6)} %and.7), kind=kLoop, calls=%fused_computation.5.clone.1 | loop fusion | flops 10480640 | bytes 10526721 | tf_op jit(solution)/shard_map/while/body/eval_jaxpr/reduce_sum | solution.py:37
  151.0 0.7 copy.50
  151.7 6.8 %fusion.40 = f32[10,512,128]{2,1,0:T(8,128)} fusion(f32[10,512,128]{2,1,0:T(8,128)} %get-tuple-element.217, bf16[512,10,128]{0,2,1:T(8,128)(2,1)S(1)} %bitcast.58, f32[10,512,512]{2,1,0:T(8,128)} %get-tuple-element.199, f32[10,512]{1,0:T(8,128)S(1)} %select_maximum_fusion.2, pred[]{:T(512)S(6)} %and.7, f32[10,512]{1,0:T(8,128)S(1)} %get-tuple-element.202, ...), kind=kOutput, calls=%fused_computation.12.clone.1 | convolution fusion | flops 683540480 | bytes 17080322 | tf_op jit(solution)/shard_map/while/body/eval_jaxpr/hqk,khd->hqd/dot_general | solution.py:38
  158.4 0.6 dynamic_slice.19
  160.3 3.0 constant_dynamic-slice_fusion.3
  163.3 1.6 copy.49
  164.9 7.0 %bitcast_reduce_fusion.2 = (f32[10,512]{1,0:T(8,128)S(1)}, f32[10,512,512]{2,1,0:T(8,128)}) fusion(pred[]{:T(512)S(6)} %and.7, bf16[512,10,128]{0,2,1:T(8,128)(2,1)S(1)} %bitcast.57, bf16[512,10,128]{2,0,1:T(8,128)(2,1)} %get-tuple-element.232), kind=kOutput, calls=%fused_computation.1.clone.1 | convolution fusion | flops 678947840 | bytes 13127681 | tf_op jit(solution)/shard_map/while/body/eval_jaxpr/qhd,khd->hqk/dot_general | solution.py:30
  171.9 6.0 %fusion.38 = f32[10,512]{1,0:T(8,128)S(1)} fusion(f32[10,512,512]{2,1,0:T(8,128)} %get-tuple-element.199, f32[10,512]{1,0:T(8,128)S(1)} %select_maximum_fusion.2, pred[]{:T(512)S(6)} %and.7), kind=kLoop, calls=%fused_computation.5.clone.1 | loop fusion | flops 10480640 | bytes 10526721 | tf_op jit(solution)/shard_map/while/body/eval_jaxpr/reduce_sum | solution.py:37
  178.0 0.7 copy.50
  178.6 7.4 %fusion.40 = f32[10,512,128]{2,1,0:T(8,128)} fusion(f32[10,512,128]{2,1,0:T(8,128)} %get-tuple-element.217, bf16[512,10,128]{0,2,1:T(8,128)(2,1)S(1)} %bitcast.58, f32[10,512,512]{2,1,0:T(8,128)} %get-tuple-element.199, f32[10,512]{1,0:T(8,128)S(1)} %select_maximum_fusion.2, pred[]{:T(512)S(6)} %and.7, f32[10,512]{1,0:T(8,128)S(1)} %get-tuple-element.202, ...), kind=kOutput, calls=%fused_computation.12.clone.1 | convolution fusion | flops 683540480 | bytes 17080322 | tf_op jit(solution)/shard_map/while/body/eval_jaxpr/hqk,khd->hqd/dot_general | solution.py:38
  186.0 0.6 dynamic_slice.19
  187.9 3.0 constant_dynamic-slice_fusion.3
  190.9 1.6 copy.49
  192.5 7.0 %bitcast_reduce_fusion.2 = (f32[10,512]{1,0:T(8,128)S(1)}, f32[10,512,512]{2,1,0:T(8,128)}) fusion(pred[]{:T(512)S(6)} %and.7, bf16[512,10,128]{0,2,1:T(8,128)(2,1)S(1)} %bitcast.57, bf16[512,10,128]{2,0,1:T(8,128)(2,1)} %get-tuple-element.232), kind=kOutput, calls=%fused_computation.1.clone.1 | convolution fusion | flops 678947840 | bytes 13127681 | tf_op jit(solution)/shard_map/while/body/eval_jaxpr/qhd,khd->hqk/dot_general | solution.py:30
  199.5 6.0 %fusion.38 = f32[10,512]{1,0:T(8,128)S(1)} fusion(f32[10,512,512]{2,1,0:T(8,128)} %get-tuple-element.199, f32[10,512]{1,0:T(8,128)S(1)} %select_maximum_fusion.2, pred[]{:T(512)S(6)} %and.7), kind=kLoop, calls=%fused_computation.5.clone.1 | loop fusion | flops 10480640 | bytes 10526721 | tf_op jit(solution)/shard_map/while/body/eval_jaxpr/reduce_sum | solution.py:37
  205.6 0.7 copy.50
  206.3 7.4 %fusion.40 = f32[10,512,128]{2,1,0:T(8,128)} fusion(f32[10,512,128]{2,1,0:T(8,128)} %get-tuple-element.217, bf16[512,10,128]{0,2,1:T(8,128)(2,1)S(1)} %bitcast.58, f32[10,512,512]{2,1,0:T(8,128)} %get-tuple-element.199, f32[10,512]{1,0:T(8,128)S(1)} %select_maximum_fusion.2, pred[]{:T(512)S(6)} %and.7, f32[10,512]{1,0:T(8,128)S(1)} %get-tuple-element.202, ...), kind=kOutput, calls=%fused_computation.12.clone.1 | convolution fusion | flops 683540480 | bytes 17080322 | tf_op jit(solution)/shard_map/while/body/eval_jaxpr/hqk,khd->hqd/dot_general | solution.py:38
  213.7 0.6 dynamic_slice.19
  215.6 3.0 constant_dynamic-slice_fusion.3
  218.5 1.6 copy.49
  220.1 7.0 %bitcast_reduce_fusion.2 = (f32[10,512]{1,0:T(8,128)S(1)}, f32[10,512,512]{2,1,0:T(8,128)}) fusion(pred[]{:T(512)S(6)} %and.7, bf16[512,10,128]{0,2,1:T(8,128)(2,1)S(1)} %bitcast.57, bf16[512,10,128]{2,0,1:T(8,128)(2,1)} %get-tuple-element.232), kind=kOutput, calls=%fused_computation.1.clone.1 | convolution fusion | flops 678947840 | bytes 13127681 | tf_op jit(solution)/shard_map/while/body/eval_jaxpr/qhd,khd->hqk/dot_general | solution.py:30
  227.1 6.0 %fusion.38 = f32[10,512]{1,0:T(8,128)S(1)} fusion(f32[10,512,512]{2,1,0:T(8,128)} %get-tuple-element.199, f32[10,512]{1,0:T(8,128)S(1)} %select_maximum_fusion.2, pred[]{:T(512)S(6)} %and.7), kind=kLoop, calls=%fused_computation.5.clone.1 | loop fusion | flops 10480640 | bytes 10526721 | tf_op jit(solution)/shard_map/while/body/eval_jaxpr/reduce_sum | solution.py:37
  233.2 0.7 copy.50
  233.9 7.4 %fusion.40 = f32[10,512,128]{2,1,0:T(8,128)} fusion(f32[10,512,128]{2,1,0:T(8,128)} %get-tuple-element.217, bf16[512,10,128]{0,2,1:T(8,128)(2,1)S(1)} %bitcast.58, f32[10,512,512]{2,1,0:T(8,128)} %get-tuple-element.199, f32[10,512]{1,0:T(8,128)S(1)} %select_maximum_fusion.2, pred[]{:T(512)S(6)} %and.7, f32[10,512]{1,0:T(8,128)S(1)} %get-tuple-element.202, ...), kind=kOutput, calls=%fused_computation.12.clone.1 | convolution fusion | flops 683540480 | bytes 17080322 | tf_op jit(solution)/shard_map/while/body/eval_jaxpr/hqk,khd->hqd/dot_general | solution.py:38
  241.3 2.1 copy.40
  243.5 1.4 divide_convert_fusion
  245.7 0.6 fusion.19
  246.4 0.6 iota_compare_fusion.4
  247.2 17.4 %all-gather.9.cloned.1.call-done = bf16[512,2560]{0,1:T(8,128)(2,1)} async-done(((bf16[512,1280]{0,1:T(8,128)(2,1)}), bf16[512,2560]{0,1:T(8,128)(2,1)}) %all-gather.9.cloned.1.call-update) | async-done | bytes 2621456 | tf_op jit(solution)/shard_map/all_gather | solution.py:63
  264.6 125.1 %all-gather.11.cloned.1.call-done = bf16[2560,2560]{1,0:T(8,128)(2,1)} async-done(((bf16[80,2560]{1,0:T(8,128)(2,1)}), bf16[2560,2560]{1,0:T(8,128)(2,1)}) %all-gather.11.cloned.1.call-update) | async-done | bytes 13107216 | tf_op jit(solution)/shard_map/all_gather | solution.py:66
  389.8 13.9 %fusion.16 = bf16[512,2560]{1,0:T(8,128)(2,1)} fusion(bf16[512,2560]{0,1:T(8,128)(2,1)} %all-gather.9.cloned.1.call-done, bf16[2560,2560]{1,0:T(8,128)(2,1)} %all-gather.11.cloned.1.call-done, bf16[1,1,512,2560]{3,2,1,0:T(8,128)(2,1)} %param.16, f32[2560]{0:T(1024)S(1)} %select_reduce_fusion), kind=kOutput, calls=%fused_computation.25 | convolution fusion | flops 6716129280 | bytes 20981760 | tf_op jit(solution)/shard_map/dot_general | solution.py:64
  403.6 3.1 reshape.46
  406.8 1.5 convolution_convert_fusion
  408.3 4.1 copy.46
  412.4 5.6 %all-to-all-start = ((bf16[32,2,16,2560]{3,2,1,0:T(8,128)(2,1)}), bf16[32,2,16,2560]{3,2,1,0:T(8,128)(2,1)}, u32[]{:S(2)}, u32[]{:S(2)}) async-start(bf16[32,2,16,2560]{3,2,1,0:T(8,128)(2,1)} %bitcast.59), calls=%async_computation | async-start | bytes 10485760 | tf_op jit(solution)/shard_map/all_to_all | solution.py:98
  418.0 115.4 %all-to-all-done = bf16[32,2,16,2560]{3,2,1,0:T(8,128)(2,1)} async-done(((bf16[32,2,16,2560]{3,2,1,0:T(8,128)(2,1)}), bf16[32,2,16,2560]{3,2,1,0:T(8,128)(2,1)}, u32[]{:S(2)}, u32[]{:S(2)}) %all-to-all-start) | async-done | bytes 5242912 | tf_op jit(solution)/shard_map/all_to_all | solution.py:98
  533.4 6.5 %fusion.15 = bf16[1,1,32,2,16,2560]{5,4,3,2,1,0:T(8,128)(2,1)} fusion(bf16[32,2,16,2560]{3,2,1,0:T(8,128)(2,1)} %all-to-all-done, f32[2560]{0:T(1024)S(1)} %copy-done.2, f32[32]{0:T(128)S(1)} %fusion.20), kind=kLoop, calls=%fused_computation.23 | loop fusion | flops 10485760 | bytes 10496128 | tf_op jit(solution)/shard_map/broadcast_in_dim | solution.py:102
  (45 shorter events, 1.4 us)
Async XLA Ops:
  6.5 1.6 copy-start
  6.5 63.0 %all-gather.5.cloned.1.call-start = ((), (), s32[]{:S(2)}) async-start(), calls=%async_computation.1 | async-start | bytes 6553600 | tf_op jit(solution)/shard_map/all_gather | solution.py:49
  7.3 124.2 %all-gather.7.cloned.1.call-start = ((), (), s32[]{:S(2)}) async-start(), calls=%async_computation.2 | async-start | bytes 6553600 | tf_op jit(solution)/shard_map/all_gather | solution.py:50
  8.0 256.6 %all-gather.9.cloned.1.call-start = ((), (), s32[]{:S(2)}) async-start(), calls=%async_computation.3 | async-start | bytes 3932160 | tf_op jit(solution)/shard_map/all_gather | solution.py:63
  243.4 2.1 copy-start.3
  243.5 2.2 copy-start.4
  243.5 3.6 copy-start.1
  244.9 144.8 %all-gather.11.cloned.1.call-start = ((), (), s32[]{:S(2)}) async-start(), calls=%async_computation.4 | async-start | bytes 13516800 | tf_op jit(solution)/shard_map/all_gather | solution.py:66
  412.4 5.6 %copy-start.6 = (f32[4]{0:T(128)S(1)}, f32[4]{0:T(128)}, u32[]{:S(2)}) copy-start(f32[4]{0:T(128)} %param.19) | copy-start | bytes 52
  412.4 5.7 %copy-start.5 = (s32[32]{0:T(128)S(1)}, s32[32]{0:T(128)}, u32[]{:S(2)}) copy-start(s32[32]{0:T(128)} %param.22) | copy-start | bytes 388
  412.4 121.0 %copy-start.2 = (f32[2560]{0:T(1024)S(1)}, f32[2560]{0:T(1024)}, u32[]{:S(2)}) copy-start(f32[2560]{0:T(1024)} %param.20) | copy-start | bytes 30724
  412.4 121.0 %all-to-all-start = ((bf16[32,2,16,2560]{3,2,1,0:T(8,128)(2,1)}), bf16[32,2,16,2560]{3,2,1,0:T(8,128)(2,1)}, u32[]{:S(2)}, u32[]{:S(2)}) async-start(bf16[32,2,16,2560]{3,2,1,0:T(8,128)(2,1)} %bitcast.59), calls=%async_computation | async-start | bytes 10485760 | tf_op jit(solution)/shard_map/all_to_all | solution.py:98
Sparse Core Ops, SparseCore 0:
  9.2 60.3 all-gather.4
  71.4 60.0 all-gather.6
  245.0 19.5 all-gather.8
  267.1 122.6 all-gather.10
where the time goes:
time: 552 us; the launch traced here: 546 us
  waiting for transfers between devices  381 us (69%)
  matrix products  72.4 us (13%)
  local copies, waits for them, and re-layouts  34.8 us (6%)
  other arithmetic  34 us (6%)
  between operations  13.3 us (2%)
  starting transfers between devices  5.87 us (1%)
    all_gather x1, waiting for transfers between devices, shards(): lax.all_gather(out_weight, 'clip', axis=0, tiled=True)  125 us
    all_to_all x1, waiting for transfers between devices, shards(): lax.all_to_all(buffer, 'clip', split_axis=0, concat_axis=0, tiled=True)  115 us
    all_gather x1, waiting for transfers between devices, shards(): val_piece = lax.all_gather(values, 'span', axis=1, tiled=True)  61.9 us
    all_gather x1, waiting for transfers between devices, shards(): key_piece = lax.all_gather(keys, 'span', axis=1, tiled=True)  59.3 us
    dot_general x4, matrix products, absorb(): jnp.einsum('hqk,khd->hqd', prob.astype(jnp.bfloat16), val_heads, preferre...  29 us
    dot_general x4, matrix products, absorb(): jnp.einsum('qhd,khd->hqk', query, key_heads, preferred_element_type=jnp.f...  28 us
    reduce_sum x4, other arithmetic, absorb(): total = total * factor + jnp.sum(prob, axis=-1)  24.2 us
    dynamic_slice x16, local copies, waits for them, and re-layouts, shards(): lax.scan(step_one, carry, (key_piece[0], val_piece[0], jnp.arange(count,...  23.3 us
  transfers between devices with their start and end apart: 5, of which 5 were waited for; matrix products, arithmetic and copies ran while one was open for 1% of the time, Pallas kernels for 0%

commit v1 on v0

v1 whole, which is shorter than its diff:
```python
import functools
import math

import jax
import jax.numpy as jnp
from jax import lax
from jax.experimental import pallas as pl
from jax.experimental.pallas import tpu as pltpu
from jax.sharding import PartitionSpec as P

MESH = pl.DeviceIdType.MESH
HS = 128
NX, NZ, NY = 4, 8, 4
NCLIP = 32
TOK = 512
NB = 32
BR = 16
HALF = 1280
INNER = 2560
WID = 2560
SHARD = 80
MAXH = 3
CA = 768
PART = {
    "A": ((0, CA), (0, CA // 2), (CA // 2, CA)),
    "B": ((CA, WID), (CA, (CA + WID) // 2), ((CA + WID) // 2, WID)),
}
CHUNKS = ((0, 256, "A"), (256, 768, "A"), (768, 1280, "B"), (1280, 1792, "B"), (1792, 2304, "B"), (2304, 2560, "B"))


def plan():
    names = []
    for way in (1, -1):
        for hop in (1, 2, 3, 4):
            names.append(("Bz", way, hop))
        for hop in (1, 2):
            names.append(("Ax", way, hop))
        for hop in (1, 2, 3, 4):
            for xrel in (0, -1, 1, 2):
                names.append(("Az", way, hop, xrel))
        for hop in (1, 2):
            for zrel in (0, -1, 1, -2, 2, -3, 3, 4):
                names.append(("Bx", way, hop, zrel))
    return {name: at for at, name in enumerate(names)}


NAMES = plan()


def kernel(
    q_ref, k_ref, v_ref, resid_ref, w_ref, gate_ref, gain_ref, scale_ref, route_ref, len_ref, step_ref,
    out_ref,
    qkv, obuf, feats, wfull, resid_v, valbuf, sendbuf, inv,
    q_send, q_recv, o_send, o_recv, sib_send, sib_recv, w_send, w_recv, w_own, r_sem, a_send, a_recv,
):
    y = lax.axis_index("span")
    cl = lax.axis_index("clip")
    m = lax.axis_index("mp")
    x = cl // NZ
    z = lax.rem(cl, NZ)

    def clip_at(dx, dz):
        return lax.rem(x + (dx + NX), NX) * NZ + lax.rem(z + (dz + NZ), NZ)

    def first_head(yy):
        return (5 * yy + 1 - m) // 2

    def has_head(yy, i):
        return first_head(yy) + i < first_head(yy + 1)

    def cols128(at):
        return pl.ds(pl.multiple_of(at * HS, HS), HS)

    def remote(src, dst, send, recv, target):
        return pltpu.make_async_remote_copy(
            src_ref=src, dst_ref=dst, send_sem=send, recv_sem=recv, device_id=target, device_id_type=MESH
        )

    barrier = pltpu.get_barrier_semaphore()

    def greet(d, carry):
        pl.semaphore_signal(
            barrier, inc=1, device_id=(y, lax.rem(cl + d, NCLIP), m), device_id_type=MESH
        )
        return carry

    lax.fori_loop(1, NCLIP, greet, 0)
    for d in (1, 2, 3):
        pl.semaphore_signal(barrier, inc=1, device_id=(lax.rem(y + d, NY), cl, m), device_id_type=MESH)
    pl.semaphore_signal(barrier, inc=1, device_id=(y, cl, 1 - m), device_id_type=MESH)
    pl.semaphore_wait(barrier, NCLIP - 1 + 3 + 1)

    waited, sent = set(), []

    def rows_of(rel):
        return pl.ds(pl.multiple_of(clip_at(*rel) * SHARD, 16), SHARD)

    def w_start(name, rel, target, half=None, own=False):
        lo, hi = PART[name[0][0]][0 if half is None else 1 + half]
        dst = wfull.at[rows_of(rel), lo:hi]
        src = w_ref.at[:, lo:hi] if own else dst
        sent.append(hi - lo)
        remote(src, dst, w_send, w_recv.at[NAMES[name]], (y, clip_at(*target), m)).start()

    def w_wait(name, rel, half=None):
        if name in waited:
            return
        waited.add(name)
        lo, hi = PART[name[0][0]][0 if half is None else 1 + half]
        dst = wfull.at[rows_of(rel), lo:hi]
        remote(dst, dst, w_send, w_recv.at[NAMES[name]], (y, cl, m)).wait_recv()

    def half_of(way):
        return 0 if way == 1 else 1

    def bz_wait(way, hop):
        w_wait(("Bz", way, hop), (0, -way * hop), half_of(way) if hop == 4 else None)

    def ax_wait(way, hop):
        w_wait(("Ax", way, hop), (-way * hop, 0), half_of(way) if hop == 2 else None)

    def az_wait(way, hop, xrel):
        w_wait(("Az", way, hop, xrel), (xrel, -way * hop), half_of(way) if hop == 4 else None)

    def bx_wait(way, hop, zrel):
        w_wait(("Bx", way, hop, zrel), (-way * hop, zrel), half_of(way) if hop == 2 else None)

    def b_to_x(zrel, own=False):
        for way in (1, -1):
            w_start(("Bx", way, 1, zrel), (0, zrel), (way, 0), own=own)

    def a_to_z(xrel, own=False):
        for way in (1, -1):
            w_start(("Az", way, 1, xrel), (xrel, 0), (0, way), own=own)

    def bz_event(hop):
        for way in (1, -1):
            bz_wait(way, hop)
            if hop < 4:
                w_start(
                    ("Bz", way, hop + 1), (0, -way * hop), (0, way), half=half_of(way) if hop == 3 else None
                )
                b_to_x(-way * hop)
        if hop == 4:
            b_to_x(4)

    def ax_event(hop):
        for way in (1, -1):
            ax_wait(way, hop)
            if hop == 1:
                w_start(("Ax", way, 2), (-way, 0), (way, 0), half=half_of(way))
                a_to_z(-way)
        if hop == 2:
            a_to_z(2)

    def az_event(hop, xrel):
        for way in (1, -1):
            az_wait(way, hop, xrel)
            w_start(
                ("Az", way, hop + 1, xrel), (xrel, -way * hop), (0, way), half=half_of(way) if hop == 3 else None
            )

    def bx_event(zrel):
        for way in (1, -1):
            bx_wait(way, 1, zrel)
            w_start(("Bx", way, 2, zrel), (-way, zrel), (way, 0), half=half_of(way))

    def all_of(part):
        for way in (1, -1):
            if part == "A":
                for hop in (1, 2):
                    ax_wait(way, hop)
                for hop in (1, 2, 3, 4):
                    for xrel in (0, -1, 1, 2):
                        az_wait(way, hop, xrel)
            else:
                for hop in (1, 2, 3, 4):
                    bz_wait(way, hop)
                for hop in (1, 2):
                    for zrel in (0, -1, 1, -2, 2, -3, 3, 4):
                        bx_wait(way, hop, zrel)

    tensors = (q_ref, k_ref, v_ref)

    def qkv_out(i, d):
        yy = lax.rem(y + d, NY)

        @pl.when(has_head(yy, i))
        def _():
            for t in range(3):
                remote(
                    tensors[t].at[:, cols128(first_head(yy) + i)],
                    qkv.at[i, y, t],
                    q_send.at[i, d],
                    q_recv.at[i, y],
                    (yy, cl, m),
                ).start()

    def qkv_here(i):
        @pl.when(has_head(y, i))
        def _():
            for t in range(3):
                pltpu.make_async_copy(
                    tensors[t].at[:, cols128(first_head(y) + i)], qkv.at[i, y, t], q_recv.at[i, y]
                ).start()

    def qkv_sent(i, d):
        yy = lax.rem(y + d, NY)

        @pl.when(has_head(yy, i))
        def _():
            remote(qkv.at[i, 0], qkv.at[i, 0], q_send.at[i, d], q_recv.at[i, 0], (yy, cl, m)).wait_send()

    def own_cols(head):
        return cols128(m * (HALF // HS) + head)

    def to_sibling(head):
        part = feats.at[:, own_cols(head)]
        remote(part, part, sib_send, sib_recv, (y, cl, 1 - m)).start()

    rows_at_once = 256

    def attend(i, c):
        @pl.when(has_head(y, i))
        def _():
            pltpu.make_async_copy(qkv.at[i, c], qkv.at[i, c], q_recv.at[i, c]).wait()

            def tile(r, carry):
                rows = pl.ds(pl.multiple_of(r * rows_at_once, rows_at_once), rows_at_once)
                query = qkv[i, c, 0, rows, :]
                scores = [
                    lax.dot_general(
                        query, qkv[i, cc, 1], (((1,), (1,)), ((), ())), preferred_element_type=jnp.float32
                    )
                    for cc in range(c + 1)
                ]
                top = scores[0]
                for part in scores[1:]:
                    top = jnp.maximum(top, part)
                top = jnp.max(top, axis=1, keepdims=True)
                acc = jnp.zeros((rows_at_once, 2 * HS), jnp.float32)
                for cc in range(c + 1):
                    prob = jnp.exp((scores[cc] - top) * (1.0 / math.sqrt(HS))).astype(jnp.bfloat16)
                    val = jnp.concatenate([qkv[i, cc, 2], jnp.ones((TOK, HS), jnp.bfloat16)], axis=1)
                    acc = acc + jnp.dot(prob, val, preferred_element_type=jnp.float32)
                obuf[i, c, rows, :] = (acc[:, :HS] / acc[:, HS:]).astype(jnp.bfloat16)
                return carry

            lax.fori_loop(0, TOK // rows_at_once, tile, 0)
            head = first_head(y) + i

            @pl.when(y == c)
            def _():
                feats[:, own_cols(head)] = obuf[i, c]
                to_sibling(head)

            @pl.when(y != c)
            def _():
                remote(
                    obuf.at[i, c], feats.at[:, own_cols(head)], o_send.at[i, c], o_recv.at[head], (c, cl, m)
                ).start()

    def o_event(i):
        for d in (1, 2, 3):
            yy = lax.rem(y + d, NY)

            @pl.when(has_head(yy, i))
            def _(yy=yy):
                head = first_head(yy) + i
                part = feats.at[:, own_cols(head)]
                remote(part, part, o_send.at[i, 0], o_recv.at[head], (y, cl, m)).wait_recv()
                to_sibling(head)

    def find_slots():
        def of_group(g, carry):
            first, second, found = jnp.int32(NB), jnp.int32(NB), jnp.int32(0)
            for b in range(NB):
                here = route_ref[b] == g
                first = jnp.where(here & (found == 0), b, first)
                second = jnp.where(here & (found == 1), b, second)
                found = found + jnp.where(here, 1, 0)
            inv[2 * g] = first
            inv[2 * g + 1] = second
            return carry

        lax.fori_loop(0, NCLIP, of_group, 0)
        valbuf[NB] = jnp.zeros((BR, valbuf.shape[2]), jnp.bfloat16)

    w_start(("Bz", 1, 1), (0, 0), (0, 1), own=True)
    w_start(("Bz", -1, 1), (0, 0), (0, -1), own=True)
    for way in (1, -1):
        w_start(("Ax", way, 1), (0, 0), (way, 0), own=True)
    b_to_x(0, own=True)
    for i in range(MAXH):
        for d in (1, 3, 2):
            qkv_out(i, d)
        qkv_here(i)
        if i == 0:
            a_to_z(0, own=True)
    own_rows = wfull.at[rows_of((0, 0)), :]
    w_copy = pltpu.make_async_copy(w_ref, own_rows, w_own)
    w_copy.start()
    resid_copy = pltpu.make_async_copy(resid_ref, resid_v, r_sem)
    resid_copy.start()

    events = [(1.0, find_slots)]
    for hop, at in ((1, 6.0), (2, 12.0), (3, 18.0), (4, 22.0)):
        events.append((at, functools.partial(bz_event, hop)))
    for hop, at in ((1, 4.0), (2, 7.0)):
        events.append((at, functools.partial(ax_event, hop)))
    for hop in (1, 2, 3):
        for n, xrel in enumerate((0, -1, 1, 2)):
            events.append((18.0 + 10.0 * (hop - 1) + 2.5 * n, functools.partial(az_event, hop, xrel)))
    for n, zrel in enumerate((0, -1, 1, -2, 2, -3, 3, 4)):
        events.append((9.0 * (n + 1), functools.partial(bx_event, zrel)))
    for i in range(MAXH):
        for c in range(NY):
            events.append((13.0 * (i + 1) + 0.7 * c, functools.partial(attend, i, c)))
        events.append((13.0 * (i + 1) + (8.0 if i < 2 else 9.0), functools.partial(o_event, i)))
    events.sort(key=lambda item: item[0])
    begin = 48.5
    late = [act for at, act in events if at > begin]
    for at, act in events:
        if at <= begin:
            act()

    half_feats = feats.at[:, pl.ds(pl.multiple_of((1 - m) * HALF, HS), HALF)]
    remote(half_feats, half_feats, sib_send, sib_recv, (y, cl, 1 - m)).wait_recv()
    w_copy.wait()
    resid_copy.wait()

    step = step_ref[cl * NY + y]
    live = jnp.where(y < len_ref[cl], 1.0, 0.0).astype(jnp.float32)
    factor = scale_ref[step] * live

    def send_chunk(n, lo, hi):
        wide = hi - lo

        def tile(r, carry):
            rows = pl.ds(pl.multiple_of(r * rows_at_once, rows_at_once), rows_at_once)
            proj = jnp.dot(feats[rows, :], wfull[:, lo:hi], preferred_element_type=jnp.float32)
            gate = gate_ref[pl.ds(step, 1), lo:hi]
            row = (resid_v[rows, lo:hi].astype(jnp.float32) + gate * proj).astype(jnp.bfloat16)
            value = (row.astype(jnp.float32) * factor * gain_ref[:, lo:hi]).astype(jnp.bfloat16)
            many = rows_at_once // BR
            valbuf[pl.ds(r * many, many), :, :wide] = value.reshape(many, BR, wide)
            return carry

        lax.fori_loop(0, TOK // rows_at_once, tile, 0)

        def pack(g):
            for k in range(2):
                sendbuf[g, k, :, lo:hi] = valbuf[inv[2 * g + k], :, :wide]

        def send(d, carry):
            g = lax.rem(cl + d, NCLIP)
            pack(g)
            remote(
                sendbuf.at[g, :, :, lo:hi],
                out_ref.at[cl, :, :, lo:hi],
                a_send.at[n],
                a_recv.at[n],
                (y, g, m),
            ).start()
            return carry

        lax.fori_loop(1, NCLIP, send, 0)
        pack(cl)
        pltpu.make_async_copy(sendbuf.at[cl, :, :, lo:hi], out_ref.at[cl, :, :, lo:hi], a_recv.at[n]).start()

    for n, (lo, hi, part) in enumerate(CHUNKS):
        if part == "B":
            while late:
                late.pop(0)()
        all_of(part)
        send_chunk(n, lo, hi)
        for _ in range(2):
            if late:
                late.pop(0)()

    assert len(waited) == len(NAMES) and sum(sent) == (NCLIP - 1) * WID
    for n, (lo, hi, part) in enumerate(CHUNKS):
        most = sendbuf.at[0 : NCLIP - 1, :, :, lo:hi]
        remote(most, most, a_send.at[n], a_recv.at[n], (y, cl, m)).wait_send()
        whole = out_ref.at[:, :, :, lo:hi]
        pltpu.make_async_copy(whole, whole, a_recv.at[n]).wait()
    most = wfull.at[0 : (NCLIP - 1) * SHARD, :]
    remote(most, most, w_send, w_recv.at[0], (y, cl, m)).wait_send()
    for i in range(MAXH):
        for d in (1, 2, 3):
            qkv_sent(i, d)
        for c in range(NY):

            @pl.when(has_head(y, i) & (y != c))
            def _(i=i, c=c):
                remote(obuf.at[i, c], obuf.at[i, c], o_send.at[i, c], o_recv.at[0], (y, cl, m)).wait_send()

    remote(half_feats, half_feats, sib_send, sib_recv, (y, cl, 1 - m)).wait_send()


def shards(queries, keys, values, resid, out_weight, gate_table, step_scale, gain, route, clip_len, tstep):
    hbm = pl.BlockSpec(memory_space=pl.ANY)
    vmem = pl.BlockSpec(memory_space=pltpu.VMEM)
    smem = pl.BlockSpec(memory_space=pltpu.SMEM)
    dma = pltpu.SemaphoreType.DMA
    bf16 = jnp.bfloat16
    scored = pl.pallas_call(
        kernel,
        out_shape=jax.ShapeDtypeStruct((NCLIP, 2, BR, WID), bf16),
        in_specs=[hbm] * 5 + [vmem] * 2 + [smem] * 4,
        out_specs=hbm,
        scratch_shapes=[
            pltpu.VMEM((MAXH, NY, 3, TOK, HS), bf16),
            pltpu.VMEM((MAXH, NY, TOK, HS), bf16),
            pltpu.VMEM((TOK, INNER), bf16),
            pltpu.VMEM((INNER, WID), bf16),
            pltpu.VMEM((TOK, WID), bf16),
            pltpu.VMEM((NB + 1, BR, 512), bf16),
            pltpu.VMEM((NCLIP, 2, BR, WID), bf16),
            pltpu.SMEM((2 * NCLIP,), jnp.int32),
            dma((MAXH, NY)),
            dma((MAXH, NY)),
            dma((MAXH, NY)),
            dma((HALF // HS,)),
            dma,
            dma,
            dma,
            dma((len(NAMES),)),
            dma,
            dma,
            dma((len(CHUNKS),)),
            dma((len(CHUNKS),)),
        ],
        compiler_params=pltpu.CompilerParams(
            collective_id=0, has_side_effects=True, vmem_limit_bytes=56 * 1024 * 1024
        ),
        cost_estimate=pl.CostEstimate(flops=12_000_000_000, bytes_accessed=20_000_000, transcendentals=8_000_000),
    )(
        queries[0, 0],
        keys[0, 0],
        values[0, 0],
        resid[0, 0],
        out_weight,
        gate_table,
        gain[None, :],
        step_scale,
        route[0, 0, :, 0],
        clip_len,
        tstep.reshape(-1),
    )
    return scored[None, None]


def solution(mesh):
    placed = (
        P("clip", "span", None, "mp"),
        P("clip", "span", None, "mp"),
        P("clip", "span", None, "mp"),
        P("clip", "span", None, "mp"),
        P("clip", "mp"),
        P(None, "mp"),
        P(),
        P("mp"),
        P("clip", "span", None, None),
        P(),
        P(),
    )
    return jax.shard_map(
        shards,
        mesh=mesh,
        in_specs=placed,
        out_specs=P("span", "clip", None, None, None, "mp"),
        check_vma=False,
    )
```

time: 552 us -> 212 us (0.38)
  waiting for transfers between devices: 381 us -> 0 us
  Pallas kernels: 0 us -> 203 us
  matrix products: 72.4 us -> 0 us
  other arithmetic: 34 us -> 0 us
  local copies, waits for them, and re-layouts: 34.8 us -> 8.11 us
  between operations: 13.3 us -> 0.01 us
  starting transfers between devices: 5.87 us -> 0 us
    all_gather x4 -> x0, waiting for transfers between devices: 264 us -> none  [the longest x1 125 us: shards(): lax.all_gather(out_weight, 'clip', axis=0, tiled=True)]
    pallas_call x0 -> x1, Pallas kernels: none -> 203 us  [shards(): pl.pallas_call(kernel, out_shape=jax.ShapeDtypeStruct((NCLIP, 2, BR, WID)...]
    all_to_all x1 -> x0, waiting for transfers between devices: 115 us -> none  [shards(): lax.all_to_all(buffer, 'clip', split_axis=0, concat_axis=0, tiled=True)]
    dot_general x10 -> x0, matrix products: 72.4 us -> none  [the longest x4 29 us: absorb(): jnp.einsum('hqk,khd->hqd', prob.astype(jnp.bfloat16), val_heads, preferre...]
    reduce_sum x9 -> x0, other arithmetic: 25.3 us -> none  [the longest x4 24.2 us: absorb(): total = total * factor + jnp.sum(prob, axis=-1)]
    dynamic_slice x16 -> x0, local copies, waits for them, and re-layouts: 23.3 us -> none  [shards(): lax.scan(step_one, carry, (key_piece[0], val_piece[0], jnp.arange(count,...]
    broadcast_in_dim x1 -> x0, other arithmetic: 6.51 us -> none  [shards(): return scored[None, None]]
    all_to_all x1 -> x0, starting transfers between devices: 5.57 us -> none  [shards(): lax.all_to_all(buffer, 'clip', split_axis=0, concat_axis=0, tiled=True)]
  transfers between devices with their start and end apart: 5 -> 0, of which waited for: 5 -> 0; matrix products, arithmetic and copies ran while one was open for 1% -> 0% of each run, Pallas kernels for 0% -> 0%
where the time goes in v1:
time: 212 us; the launch traced here: 211 us
  Pallas kernels  203 us (96%)
  local copies, waits for them, and re-layouts  8.11 us (4%)
    pallas_call x1, Pallas kernels, shards(): pl.pallas_call(kernel, out_shape=jax.ShapeDtypeStruct((NCLIP, 2, BR, WID)...  203 us
    unnamed x2, local copies, waits for them, and re-layouts  6.15 us

profile of v1, /device:TPU:25, one launch (start us, length us, event | category | flops | bytes accessed | tf_op | source)
XLA Modules:
  0.0 211.3 jit_solution(1191942419932051462)
XLA Ops:
  0.0 1.3 broadcast_in_dim.6.gain_ref
  1.3 0.8 copy.13
  2.1 0.6 reshape.3.step_ref
  2.7 203.2 %shard_map.109 = bf16[32,2,16,2560]{3,2,1,0:T(8,128)(2,1)} custom-call(bf16[512,1280]{1,0:T(8,128)(2,1)} %bitcast.8, bf16[512,1280]{1,0:T(8,128)(2,1)} %bitcast.9, bf16[512,1280]{1,0:T(8,128)(2,1)} %bitcast.10, bf16[512,2560]{1,0:T(8,128)(2,1)} %bitcast.7, bf16[80,2560]{1,0:T(8,128)(2,1)} %w_ref.1, f32[4,2560]{1,0:T(4,128)} %gate_ref.1, ...), custom_call_target="tpu_custom_call" | custom-call | flops 12000000000 | bytes 20000000 | tf_op jit(solution)/shard_map/pallas_call | solution.py:407
  205.9 5.4 %copy.15 = bf16[1,1,32,2,16,2560]{5,4,3,2,1,0:T(8,128)(2,1)} copy(bf16[1,1,32,2,16,2560]{5,4,3,2,1,0:T(8,128)(2,1)} %bitcast.6) | data formatting | bytes 10485760

commit v2 on v1

v2 whole, which is shorter than its diff:
```python
import functools
import math

import jax
import jax.numpy as jnp
from jax import lax
from jax.experimental import pallas as pl
from jax.experimental.pallas import tpu as pltpu
from jax.sharding import PartitionSpec as P

MESH = pl.DeviceIdType.MESH
HS = 128
NX, NZ, NY = 4, 8, 4
NCLIP = 32
TOK = 512
NB = 32
BR = 16
HALF = 1280
HEADS = 10
INNER = 2560
WID = 2560
SHARD = 80
MAXH = 3
CAP = 3
TAB = 2 * NCLIP + 16
CA = 1024
PART = {
    "A": ((0, CA), (0, CA // 2), (CA // 2, CA)),
    "B": ((CA, WID), (CA, (CA + WID) // 2), ((CA + WID) // 2, WID)),
}
CHUNK = 512
CHUNKS = tuple((lo, lo + CHUNK) for lo in range(0, WID, CHUNK))
ROWS = 256
ZRELS = (0, -1, 1, -2, 2, -3, 3, 4)
XRELS = (0, -1, 1, 2)


def plan():
    names = []
    for way in (1, -1):
        names += [("Bz", way, hop) for hop in (1, 2, 3, 4)]
        names += [("Ax", way, hop) for hop in (1, 2)]
        names += [("Az", way, hop, xrel) for hop in (1, 2, 3, 4) for xrel in XRELS]
        names += [("Bx", way, hop, zrel) for hop in (1, 2) for zrel in ZRELS]
    return {name: at for at, name in enumerate(names)}


NAMES = plan()
RING = {
    name: at
    for at, name in enumerate(
        [(way, hop, piece) for way in (1, -1) for hop in (1, 2, 3) for piece in (0, 1)] + [(1, 4, 0), (-1, 4, 1)]
    )
}


def remote(src, dst, send, recv, target):
    return pltpu.make_async_remote_copy(
        src_ref=src, dst_ref=dst, send_sem=send, recv_sem=recv, device_id=target, device_id_type=MESH
    )


def place():
    y = lax.axis_index("span")
    cl = lax.axis_index("clip")
    m = lax.axis_index("mp")
    return y, cl, m, cl // NZ, lax.rem(cl, NZ)


def tile_rows(r):
    return pl.ds(pl.multiple_of(r * ROWS, ROWS), ROWS)


def gather_kernel(
    q_ref, k_ref, v_ref, w_ref, route_ref,
    feats, wfull, table, codes, most_ref,
    qkv, obuf, tiles, ytiles,
    q_send, q_recv, o_send, o_recv, o_here, sib_send, sib_recv, w_send, w_recv, w_own,
    t_send, t_recv, y_send, y_recv,
):
    y, cl, m, x, z = place()

    def clip_at(dx, dz):
        return lax.rem(x + (dx + NX), NX) * NZ + lax.rem(z + (dz + NZ), NZ)

    def first_head(yy):
        return (5 * yy + 1 - m) // 2

    def has_head(yy, i):
        return first_head(yy) + i < first_head(yy + 1)

    def cols128(at):
        return pl.ds(pl.multiple_of(at * HS, HS), HS)

    barrier = pltpu.get_barrier_semaphore()

    def greet(d, carry):
        pl.semaphore_signal(
            barrier, inc=1, device_id=(y, lax.rem(cl + d, NCLIP), m), device_id_type=MESH
        )
        return carry

    lax.fori_loop(1, NCLIP, greet, 0)
    for d in (1, 2, 3):
        pl.semaphore_signal(barrier, inc=1, device_id=(lax.rem(y + d, NY), cl, m), device_id_type=MESH)
    pl.semaphore_signal(barrier, inc=1, device_id=(y, cl, 1 - m), device_id_type=MESH)
    pl.semaphore_wait(barrier, NCLIP - 1 + 3 + 1)

    waited, sent = set(), []

    def rows_of(rel):
        return pl.ds(pl.multiple_of(clip_at(*rel) * SHARD, 16), SHARD)

    def w_start(name, rel, target, half=None, own=False):
        lo, hi = PART[name[0][0]][0 if half is None else 1 + half]
        dst = wfull.at[rows_of(rel), lo:hi]
        src = w_ref.at[:, lo:hi] if own else dst
        sent.append(hi - lo)
        remote(src, dst, w_send, w_recv.at[NAMES[name]], (y, clip_at(*target), m)).start()

    def w_wait(name, rel, half=None):
        if name in waited:
            return
        waited.add(name)
        lo, hi = PART[name[0][0]][0 if half is None else 1 + half]
        dst = wfull.at[rows_of(rel), lo:hi]
        remote(dst, dst, w_send, w_recv.at[NAMES[name]], (y, cl, m)).wait_recv()

    def half_of(way):
        return 0 if way == 1 else 1

    def bz_wait(way, hop):
        w_wait(("Bz", way, hop), (0, -way * hop), half_of(way) if hop == 4 else None)

    def ax_wait(way, hop):
        w_wait(("Ax", way, hop), (-way * hop, 0), half_of(way) if hop == 2 else None)

    def az_wait(way, hop, xrel):
        w_wait(("Az", way, hop, xrel), (xrel, -way * hop), half_of(way) if hop == 4 else None)

    def bx_wait(way, hop, zrel):
        w_wait(("Bx", way, hop, zrel), (-way * hop, zrel), half_of(way) if hop == 2 else None)

    def b_to_x(zrel, own=False):
        for way in (1, -1):
            w_start(("Bx", way, 1, zrel), (0, zrel), (way, 0), own=own)

    def a_to_z(xrel, own=False):
        for way in (1, -1):
            w_start(("Az", way, 1, xrel), (xrel, 0), (0, way), own=own)

    def bz_event(hop):
        for way in (1, -1):
            bz_wait(way, hop)
            if hop < 4:
                w_start(
                    ("Bz", way, hop + 1), (0, -way * hop), (0, way), half=half_of(way) if hop == 3 else None
                )
                b_to_x(-way * hop)
        if hop == 4:
            b_to_x(4)

    def ax_event(hop):
        for way in (1, -1):
            ax_wait(way, hop)
            if hop == 1:
                w_start(("Ax", way, 2), (-way, 0), (way, 0), half=half_of(way))
                a_to_z(-way)
        if hop == 2:
            a_to_z(2)

    def az_event(hop, xrel):
        for way in (1, -1):
            az_wait(way, hop, xrel)
            w_start(
                ("Az", way, hop + 1, xrel), (xrel, -way * hop), (0, way), half=half_of(way) if hop == 3 else None
            )

    def bx_event(zrel):
        for way in (1, -1):
            bx_wait(way, 1, zrel)
            w_start(("Bx", way, 2, zrel), (-way, zrel), (way, 0), half=half_of(way))

    def all_rows():
        for way in (1, -1):
            for hop in (1, 2):
                ax_wait(way, hop)
                for zrel in ZRELS:
                    bx_wait(way, hop, zrel)
            for hop in (1, 2, 3, 4):
                bz_wait(way, hop)
                for xrel in XRELS:
                    az_wait(way, hop, xrel)

    tensors = (q_ref, k_ref, v_ref)

    def qkv_out(i, d):
        yy = lax.rem(y + d, NY)

        @pl.when(has_head(yy, i))
        def _():
            for t in range(3):
                remote(
                    tensors[t].at[:, cols128(first_head(yy) + i)],
                    qkv.at[i, y, t],
                    q_send.at[i, d],
                    q_recv.at[i, y],
                    (yy, cl, m),
                ).start()

    def qkv_here(i):
        @pl.when(has_head(y, i))
        def _():
            for t in range(3):
                pltpu.make_async_copy(
                    tensors[t].at[:, cols128(first_head(y) + i)], qkv.at[i, y, t], q_recv.at[i, y]
                ).start()

    def qkv_sent(i, d):
        yy = lax.rem(y + d, NY)

        @pl.when(has_head(yy, i))
        def _():
            remote(qkv.at[i, 0], qkv.at[i, 0], q_send.at[i, d], q_recv.at[i, 0], (yy, cl, m)).wait_send()

    def own_cols(head):
        return cols128(m * HEADS + head)

    def attend(i, c):
        @pl.when(has_head(y, i))
        def _():
            pltpu.make_async_copy(qkv.at[i, c], qkv.at[i, c], q_recv.at[i, c]).wait()

            def tile(r, carry):
                rows = tile_rows(r)
                query = qkv[i, c, 0, rows, :]
                scores = [
                    lax.dot_general(
                        query, qkv[i, cc, 1], (((1,), (1,)), ((), ())), preferred_element_type=jnp.float32
                    )
                    for cc in range(c + 1)
                ]
                top = scores[0]
                for part in scores[1:]:
                    top = jnp.maximum(top, part)
                top = jnp.max(top, axis=1, keepdims=True)
                to_two = 1.0 / (math.sqrt(HS) * math.log(2.0))
                acc = jnp.zeros((ROWS, 2 * HS), jnp.float32)
                for cc in range(c + 1):
                    prob = jnp.exp2((scores[cc] - top) * to_two).astype(jnp.bfloat16)
                    val = jnp.concatenate([qkv[i, cc, 2], jnp.ones((TOK, HS), jnp.bfloat16)], axis=1)
                    acc = acc + jnp.dot(prob, val, preferred_element_type=jnp.float32)
                obuf[i, c, rows, :] = (acc[:, :HS] / acc[:, HS:]).astype(jnp.bfloat16)
                return carry

            lax.fori_loop(0, TOK // ROWS, tile, 0)
            head = first_head(y) + i
            part = feats.at[:, own_cols(head)]

            @pl.when(y == c)
            def _():
                pltpu.make_async_copy(obuf.at[i, c], part, o_here.at[i]).start()
                remote(obuf.at[i, c], part, sib_send, sib_recv, (y, cl, 1 - m)).start()

            @pl.when(y != c)
            def _():
                remote(obuf.at[i, c], part, o_send.at[i, c], o_recv.at[head], (c, cl, m)).start()

    def o_event(i):
        for d in (1, 3, 2):
            yy = lax.rem(y + d, NY)

            @pl.when(has_head(yy, i))
            def _(yy=yy):
                head = first_head(yy) + i
                part = feats.at[:, own_cols(head)]
                remote(part, part, o_send.at[i, 0], o_recv.at[head], (y, cl, m)).wait_recv()
                remote(part, part, sib_send, sib_recv, (y, cl, 1 - m)).start()

    def find_slots():
        shape = tiles.shape[1:]
        row_at = lax.broadcasted_iota(jnp.int32, shape, 0)
        lane_at = lax.broadcasted_iota(jnp.int32, shape, 1)

        def of_group(g, carry):
            count, tile = carry
            first, second, found = jnp.int32(NB), jnp.int32(NB), jnp.int32(0)
            for b in range(NB):
                here = route_ref[b] == g
                first = jnp.where(here & (found == 0), b, first)
                second = jnp.where(here & (found == 1), b, second)
                found = found + jnp.where(here, 1, 0)
            table[2 * g] = first
            table[2 * g + 1] = second
            code = jnp.where((second < NB) & (count < CAP), count, CAP)
            tile = jnp.where((row_at == 0) & (lane_at == g), code, tile)
            return count + jnp.where(second < NB, 1, 0), tile

        count, tile = lax.fori_loop(0, NCLIP, of_group, (jnp.int32(0), jnp.zeros(shape, jnp.int32)))
        tiles[cl] = jnp.where(row_at == 1, count, tile)

        def extra(e, carry):
            def look(g, carry):
                at, seen = carry
                second = table[2 * g + 1]
                have = second < NB
                at = jnp.where(have & (seen == e), second, at)
                return at, seen + jnp.where(have, 1, 0)

            at, seen = lax.fori_loop(0, NCLIP, look, (jnp.int32(0), jnp.int32(0)))
            table[2 * NCLIP + e] = at
            return carry

        lax.fori_loop(0, TAB - 2 * NCLIP, extra, 0)

        def tell(d, carry):
            g = lax.rem(cl + d, NCLIP)
            remote(tiles.at[cl], tiles.at[cl], t_send, t_recv, (y, g, m)).start()
            return carry

        lax.fori_loop(1, NCLIP, tell, 0)

    def share_most():
        others = tiles.at[0 : NCLIP - 1]
        remote(others, others, t_send, t_recv, (y, cl, m)).wait_recv()
        codes[...] = tiles[:, 0, :]
        ytiles[y] = jnp.max(tiles[...], axis=0)
        for d in (1, 2, 3):
            remote(ytiles.at[y], ytiles.at[y], y_send.at[d], y_recv.at[y], (lax.rem(y + d, NY), cl, m)).start()

    def know_most():
        for d in (1, 2, 3):
            yy = lax.rem(y + d, NY)
            remote(ytiles.at[yy], ytiles.at[yy], y_send.at[d], y_recv.at[yy], (y, cl, m)).wait_recv()
        most_ref[...] = jnp.max(ytiles[...], axis=0)

    w_start(("Bz", 1, 1), (0, 0), (0, 1), own=True)
    w_start(("Bz", -1, 1), (0, 0), (0, -1), own=True)
    for way in (1, -1):
        w_start(("Ax", way, 1), (0, 0), (way, 0), own=True)
    b_to_x(0, own=True)
    for i in range(MAXH):
        for d in (1, 3, 2):
            qkv_out(i, d)
        qkv_here(i)
        if i == 0:
            a_to_z(0, own=True)
    w_copy = pltpu.make_async_copy(w_ref, wfull.at[rows_of((0, 0)), :], w_own)
    w_copy.start()

    events = [(1.0, find_slots), (24.0, share_most), (32.0, know_most)]
    for hop, at in ((1, 5.5), (2, 11.0), (3, 16.5), (4, 20.0)):
        events.append((at, functools.partial(bz_event, hop)))
    for hop, at in ((1, 4.0), (2, 7.0)):
        events.append((at, functools.partial(ax_event, hop)))
    for hop in (1, 2, 3):
        for n, xrel in enumerate(XRELS):
            events.append((17.0 + 13.0 * (hop - 1) + 3.3 * n, functools.partial(az_event, hop, xrel)))
    for n, zrel in enumerate(ZRELS):
        events.append((7.6 * (n + 1), functools.partial(bx_event, zrel)))
    for i, at, back in ((0, 17.0, 27.0), (1, 35.0, 45.0), (2, 50.0, 61.0)):
        for c in range(NY):
            events.append((at + 0.7 * c, functools.partial(attend, i, c)))
        events.append((back, functools.partial(o_event, i)))
    events.sort(key=lambda item: item[0])
    for at, act in events:
        act()
    all_rows()

    assert len(waited) == len(NAMES) and sum(sent) == (NCLIP - 1) * WID
    w_copy.wait()
    half_feats = feats.at[:, pl.ds(pl.multiple_of((1 - m) * HALF, HS), HALF)]
    remote(half_feats, half_feats, sib_send, sib_recv, (y, cl, 1 - m)).wait()
    most = wfull.at[0 : (NCLIP - 1) * SHARD, :]
    remote(most, most, w_send, w_recv.at[0], (y, cl, m)).wait_send()
    others = tiles.at[0 : NCLIP - 1]
    remote(others, others, t_send, t_recv, (y, cl, m)).wait_send()
    for d in (1, 2, 3):
        remote(ytiles.at[0], ytiles.at[0], y_send.at[d], y_recv.at[0], (y, cl, m)).wait_send()
    for i in range(MAXH):
        for d in (1, 2, 3):
            qkv_sent(i, d)

        @pl.when(has_head(y, i))
        def _(i=i):
            part = feats.at[:, own_cols(first_head(y) + i)]
            pltpu.make_async_copy(obuf.at[i, 0], part, o_here.at[i]).wait()

        for c in range(NY):

            @pl.when(has_head(y, i) & (y != c))
            def _(i=i, c=c):
                remote(obuf.at[i, c], obuf.at[i, c], o_send.at[i, c], o_recv.at[0], (y, cl, m)).wait_send()


def greet_clips(y, cl, m):
    barrier = pltpu.get_barrier_semaphore()

    def greet(d, carry):
        pl.semaphore_signal(
            barrier, inc=1, device_id=(y, lax.rem(cl + d, NCLIP), m), device_id_type=MESH
        )
        return carry

    lax.fori_loop(1, NCLIP, greet, 0)
    return barrier


def load_all(feats_ref, w_ref, resid_ref, feats, wfull, resid, f_sem, w_sem, r_sem):
    pltpu.make_async_copy(feats_ref, feats, f_sem).start()
    loads = []
    for n, (lo, hi) in enumerate(CHUNKS):
        loads.append(pltpu.make_async_copy(w_ref.at[:, lo:hi], wfull.at[:, lo:hi], w_sem.at[n]))
        loads[n].start()
        if n == 0:
            pltpu.make_async_copy(resid_ref, resid, r_sem).start()
    ready = set()

    def wait(n):
        if not ready:
            pltpu.make_async_copy(feats_ref, feats, f_sem).wait()
            pltpu.make_async_copy(resid_ref, resid, r_sem).wait()
        if n not in ready:
            ready.add(n)
            loads[n].wait()

    return wait


def values_of(feat, resid, wfull, gate_ref, gain_ref, step, factor, lo, hi):
    proj = jnp.dot(feat, wfull[:, lo:hi], preferred_element_type=jnp.float32)
    gate = gate_ref[pl.ds(step, 1), lo:hi]
    row = (resid.astype(jnp.float32) + gate * proj).astype(jnp.bfloat16)
    return (row.astype(jnp.float32) * factor * gain_ref[:, lo:hi]).astype(jnp.bfloat16)


def step_and_factor(step_ref, len_ref, scale_ref, cl, y):
    step = step_ref[cl * NY + y]
    live = jnp.where(y < len_ref[cl], 1.0, 0.0).astype(jnp.float32)
    return step, scale_ref[step] * live


def project(valbuf, feats, resid, wfull, gate_ref, gain_ref, step, factor, lo, hi):
    many = ROWS // BR

    def tile(r, carry):
        blocks = pl.ds(r * many, many)
        value = values_of(
            feats[blocks].reshape(ROWS, INNER),
            resid[blocks, :, lo:hi].reshape(ROWS, hi - lo),
            wfull, gate_ref, gain_ref, step, factor, lo, hi,
        )
        valbuf[blocks] = value.reshape(many, BR, hi - lo)
        return carry

    lax.fori_loop(0, TOK // ROWS, tile, 0)


def padded_kernel(
    feats_ref, w_ref, resid_ref, gate_ref, gain_ref, scale_ref, table, codes, len_ref, step_ref,
    out_ref,
    feats, wfull, resid, valbuf, sendbuf,
    f_sem, w_sem, r_sem, a_send, a_recv,
):
    y, cl, m, x, z = place()
    barrier = greet_clips(y, cl, m)
    wait = load_all(feats_ref, w_ref, resid_ref, feats, wfull, resid, f_sem, w_sem, r_sem)
    step, factor = step_and_factor(step_ref, len_ref, scale_ref, cl, y)
    valbuf[NB] = jnp.zeros((BR, CHUNK), jnp.bfloat16)
    for n, (lo, hi) in enumerate(CHUNKS):
        wait(n)
        project(valbuf, feats, resid, wfull, gate_ref, gain_ref, step, factor, lo, hi)
        if n == 0:
            pl.semaphore_wait(barrier, NCLIP - 1)

        def pack(g):
            for k in range(2):
                sendbuf[g, k, :, lo:hi] = valbuf[table[2 * g + k]]

        def send(d, carry):
            g = lax.rem(cl + d, NCLIP)
            pack(g)
            remote(
                sendbuf.at[g, :, :, lo:hi], out_ref.at[cl, :, :, lo:hi], a_send.at[n], a_recv.at[n], (y, g, m)
            ).start()
            return carry

        lax.fori_loop(1, NCLIP, send, 0)
        pack(cl)
        pltpu.make_async_copy(sendbuf.at[cl, :, :, lo:hi], out_ref.at[cl, :, :, lo:hi], a_recv.at[n]).start()
    for n, (lo, hi) in enumerate(CHUNKS):
        most = sendbuf.at[0 : NCLIP - 1, :, :, lo:hi]
        remote(most, most, a_send.at[n], a_recv.at[n], (y, cl, m)).wait_send()
        whole = out_ref.at[:, :, :, lo:hi]
        pltpu.make_async_copy(whole, whole, a_recv.at[n]).wait()


def short_kernel(
    feats_ref, w_ref, resid_ref, gate_ref, gain_ref, scale_ref, table, codes, len_ref, step_ref,
    out_ref,
    feats, wfull, resid, valbuf, sendbuf, featx, ext, stage, sendx,
    f_sem, w_sem, r_sem, a_send, a_recv, e_send, e_recv, x_send, x_recv,
):
    y, cl, m, x, z = place()
    barrier = greet_clips(y, cl, m)
    wait = load_all(feats_ref, w_ref, resid_ref, feats, wfull, resid, f_sem, w_sem, r_sem)
    step, factor = step_and_factor(step_ref, len_ref, scale_ref, cl, y)
    valbuf[NB] = jnp.zeros((BR, CHUNK), jnp.bfloat16)
    stage[CAP] = jnp.zeros((BR, WID), jnp.bfloat16)

    def firsts(n):
        lo, hi = CHUNKS[n]
        wait(n)
        project(valbuf, feats, resid, wfull, gate_ref, gain_ref, step, factor, lo, hi)
        if n == 0:
            pl.semaphore_wait(barrier, NCLIP - 1)

        def send(d, carry):
            g = lax.rem(cl + d, NCLIP)
            sendbuf[g, :, lo:hi] = valbuf[table[2 * g]]
            remote(
                sendbuf.at[g, :, lo:hi], out_ref.at[cl, 0, :, lo:hi], a_send.at[n], a_recv.at[n], (y, g, m)
            ).start()
            return carry

        lax.fori_loop(1, NCLIP, send, 0)
        sendbuf[cl, :, lo:hi] = valbuf[table[2 * cl]]
        pltpu.make_async_copy(sendbuf.at[cl, :, lo:hi], out_ref.at[cl, 0, :, lo:hi], a_recv.at[n]).start()

    pieces = ((0, WID // 2), (WID // 2, WID))

    def z_at(dz):
        return lax.rem(z + (dz + NZ), NZ)

    def ring_start(way, hop, piece):
        lo, hi = pieces[piece]
        part = ext.at[z_at(-way * (hop - 1)), :, :, lo:hi]
        remote(part, part, e_send, e_recv.at[RING[way, hop, piece]], (y, x * NZ + z_at(way), m)).start()

    def ring_wait(way, hop, piece):
        lo, hi = pieces[piece]
        part = ext.at[z_at(-way * hop), :, :, lo:hi]
        remote(part, part, e_send, e_recv.at[RING[way, hop, piece]], (y, cl, m)).wait_recv()

    def to_x(zrel):
        zs = z_at(zrel)
        source = x * NZ + zs
        stage[0:CAP] = ext[zs]
        for d in (1, 3, 2, 0):
            xx = lax.rem(x + d, NX)
            g = xx * NZ + z
            sendx[xx, zs] = stage[codes[source, g]]
            if d:
                remote(sendx.at[xx, zs], out_ref.at[source, 1], x_send, x_recv, (y, g, m)).start()
            else:
                pltpu.make_async_copy(sendx.at[xx, zs], out_ref.at[source, 1], x_recv).start()

    def seconds():
        blocks = [table[2 * NCLIP + e] for e in range(CAP)]
        for e in range(CAP):
            featx[e * BR : (e + 1) * BR, :] = feats[blocks[e]]
        for n, (lo, hi) in enumerate(CHUNKS):
            wait(n)
            left = jnp.concatenate([resid[blocks[e], :, lo:hi] for e in range(CAP)], axis=0)
            value = values_of(featx[...], left, wfull, gate_ref, gain_ref, step, factor, lo, hi)
            ext[z, :, :, lo:hi] = value.reshape(CAP, BR, hi - lo)
            for piece in (0, 1):
                if lo < pieces[piece][1] <= hi:
                    for way in (1, -1):
                        ring_start(way, 1, piece)
        to_x(0)

    def ring_event(hop):
        for piece in (0, 1):
            for way in (1, -1):
                if (way, hop, piece) in RING:
                    ring_wait(way, hop, piece)
                    if (way, hop + 1, piece) in RING:
                        ring_start(way, hop + 1, piece)
        if hop < 4:
            to_x(-hop)
            to_x(hop)
        else:
            to_x(4)

    firsts(0)
    seconds()
    firsts(1)
    ring_event(1)
    firsts(2)
    ring_event(2)
    firsts(3)
    ring_event(3)
    firsts(4)
    ring_event(4)

    for n, (lo, hi) in enumerate(CHUNKS):
        most = sendbuf.at[0 : NCLIP - 1, :, lo:hi]
        remote(most, most, a_send.at[n], a_recv.at[n], (y, cl, m)).wait_send()
        whole = out_ref.at[:, 0, :, lo:hi]
        pltpu.make_async_copy(whole, whole, a_recv.at[n]).wait()
    most = ext.at[0 : NZ - 1]
    remote(most, most, e_send, e_recv.at[0], (y, cl, m)).wait_send()
    most = sendx.at[0 : NX - 1]
    remote(most, most, x_send, x_recv, (y, cl, m)).wait_send()
    whole = out_ref.at[:, 1]
    pltpu.make_async_copy(whole, whole, x_recv).wait()


def shards(queries, keys, values, resid, out_weight, gate_table, step_scale, gain, route, clip_len, tstep):
    any_place = pl.BlockSpec(memory_space=pl.ANY)
    hbm = pl.BlockSpec(memory_space=pltpu.HBM)
    vmem = pl.BlockSpec(memory_space=pltpu.VMEM)
    smem = pl.BlockSpec(memory_space=pltpu.SMEM)
    dma = pltpu.SemaphoreType.DMA
    bf16, i32 = jnp.bfloat16, jnp.int32
    shape = jax.ShapeDtypeStruct
    feats, wfull, table, codes, most = pl.pallas_call(
        gather_kernel,
        out_shape=(
            shape((TOK, INNER), bf16),
            shape((INNER, WID), bf16),
            shape((TAB,), i32),
            shape((NCLIP, 128), i32),
            shape((8, 128), i32),
        ),
        in_specs=[hbm] * 4 + [smem],
        out_specs=(any_place, hbm, smem, vmem, vmem),
        scratch_shapes=[
            pltpu.VMEM((MAXH, NY, 3, TOK, HS), bf16),
            pltpu.VMEM((MAXH, NY, TOK, HS), bf16),
            pltpu.VMEM((NCLIP, 8, 128), i32),
            pltpu.VMEM((NY, 8, 128), i32),
            dma((MAXH, NY)),
            dma((MAXH, NY)),
            dma((MAXH, NY)),
            dma((HEADS,)),
            dma((MAXH,)),
            dma,
            dma,
            dma,
            dma((len(NAMES),)),
            dma,
            dma,
            dma,
            dma((NY,)),
            dma((NY,)),
        ],
        compiler_params=pltpu.CompilerParams(
            collective_id=0, has_side_effects=True, vmem_limit_bytes=58 * 1024 * 1024
        ),
        cost_estimate=pl.CostEstimate(flops=4_000_000_000, bytes_accessed=40_000_000, transcendentals=8_000_000),
    )(queries[0, 0], keys[0, 0], values[0, 0], out_weight, route[0, 0, :, 0])

    def exchange(kernel, number, scratch):
        return pl.pallas_call(
            kernel,
            out_shape=shape((NCLIP, 2, BR, WID), bf16),
            in_specs=[any_place, hbm, hbm] + [vmem] * 2 + [smem] * 5,
            out_specs=any_place,
            scratch_shapes=[
                pltpu.VMEM((NB, BR, INNER), bf16),
                pltpu.VMEM((INNER, WID), bf16),
                pltpu.VMEM((NB, BR, WID), bf16),
                pltpu.VMEM((NB + 1, BR, CHUNK), bf16),
            ]
            + scratch,
            compiler_params=pltpu.CompilerParams(
                collective_id=number, has_side_effects=True, vmem_limit_bytes=50 * 1024 * 1024
            ),
            cost_estimate=pl.CostEstimate(flops=7_000_000_000, bytes_accessed=30_000_000, transcendentals=0),
        )

    loads = [dma, dma((len(CHUNKS),)), dma]
    by_chunk = [dma((len(CHUNKS),)), dma((len(CHUNKS),))]
    short = exchange(
        short_kernel,
        1,
        [
            pltpu.VMEM((NCLIP, BR, WID), bf16),
            pltpu.VMEM((CAP * BR, INNER), bf16),
            pltpu.VMEM((NZ, CAP, BR, WID), bf16),
            pltpu.VMEM((CAP + 1, BR, WID), bf16),
            pltpu.VMEM((NX, NZ, BR, WID), bf16),
        ]
        + loads
        + by_chunk
        + [dma, dma((len(RING),)), dma, dma],
    )
    padded = exchange(padded_kernel, 2, [pltpu.VMEM((NCLIP, 2, BR, WID), bf16)] + loads + by_chunk)
    scored = lax.cond(
        most[1, 0] <= CAP,
        short,
        padded,
        feats.reshape(NB, BR, INNER),
        wfull,
        resid[0, 0].reshape(NB, BR, WID),
        gate_table,
        gain[None, :],
        step_scale,
        table,
        codes,
        clip_len,
        tstep.reshape(-1),
    )
    return scored[None, None]


def solution(mesh):
    placed = (
        P("clip", "span", None, "mp"),
        P("clip", "span", None, "mp"),
        P("clip", "span", None, "mp"),
        P("clip", "span", None, "mp"),
        P("clip", "mp"),
        P(None, "mp"),
        P(),
        P("mp"),
        P("clip", "span", None, None),
        P(),
        P(),
    )
    return jax.shard_map(
        shards,
        mesh=mesh,
        in_specs=placed,
        out_specs=P("span", "clip", None, None, None, "mp"),
        check_vma=False,
    )
```

time: 212 us -> 219 us (1.033)
  Pallas kernels: 203 us -> 212 us
  local copies, waits for them, and re-layouts: 8.11 us -> 5.15 us
    pallas_call x1 -> x2, Pallas kernels: 203 us -> 212 us  [the longest x1 119 us: shards(): lax.cond(most[1, 0] <= CAP, short, padded, feats.reshape(NB, BR, INNER),...]
    unnamed x2 -> x10, local copies, waits for them, and re-layouts: 6.15 us -> 3.15 us
where the time goes in v2:
time: 219 us; the launch traced here: 218 us
  Pallas kernels  212 us (97%)
  local copies, waits for them, and re-layouts  5.15 us (2%)
    pallas_call x1, Pallas kernels, shards(): lax.cond(most[1, 0] <= CAP, short, padded, feats.reshape(NB, BR, INNER),...  119 us
    pallas_call x1, Pallas kernels, shards(): pl.pallas_call(gather_kernel, out_shape=(shape((TOK, INNER), bf16), shape...  93.3 us

profile of v2, /device:TPU:25, one launch (start us, length us, event | category | flops | bytes accessed | tf_op | source)
XLA Modules:
  0.0 218.2 jit_solution(14130917252038813053)
XLA Ops:
  0.0 0.7 broadcast_in_dim.10
  0.7 0.8 copy.15
  1.5 0.1 reshape.11
  1.6 0.0 copy-start
  1.6 0.0 copy-start.1
  1.6 0.0 copy-start.2
  1.6 0.0 copy-start.3
  1.6 93.3 %shard_map.111 = (bf16[512,2560]{1,0:T(8,128)(2,1)S(1)}, bf16[2560,2560]{1,0:T(8,128)(2,1)}, s32[80]{0:T(128)S(1)}, s32[32,128]{1,0:T(8,128)S(1)}, s32[8,128]{1,0:T(8,128)}) custom-call(bf16[512,1280]{1,0:T(8,128)(2,1)} %bitcast.13, bf16[512,1280]{1,0:T(8,128)(2,1)} %bitcast.14, bf16[512,1280]{1,0:T(8,128)(2,1)} %bitcast.15, bf16[80,2560]{1,0:T(8,128)(2,1)} %w_ref.1, ...), custom_call_target="tpu_custom_call" | custom-call | flops 4000000000 | bytes 40000000 | tf_op jit(solution)/shard_map/pallas_call | solution.py:618
  94.9 1.2 slice.3
  96.7 0.0 copy-done
  96.7 0.0 copy-done.1
  96.8 0.0 copy-done.2
  96.8 0.0 copy-done.3
  96.8 119.0 %conditional.1 = (bf16[1,1,32,2,16,2560]{5,4,3,2,1,0:T(8,128)(2,1)S(1)}) conditional(s32[]{:T(128)} %bitcast.6, (bf16[32,16,2560]{2,1,0:T(8,128)(2,1)S(1)}, bf16[2560,2560]{1,0:T(8,128)(2,1)}, bf16[32,16,2560]{2,1,0:T(8,128)(2,1)S(1)}, f32[4,2560]{1,0:T(4,128)S(1)}, f32[1,2560]{1,0:T(1,128)S(1)}, /*index=5*/f32[4]{0:T(128)S(1)}, s32[80]{0:T(128)S(1)}, ...), branch_computations={%region_0.0_spmd, %region_1.0_spmd} | conditional | flops 7000000000 | bytes 30000008 | solution.py:691
  97.0 118.8 %branch_0_fun.1 = bf16[32,2,16,2560]{3,2,1,0:T(8,128)(2,1)S(1)} custom-call(bf16[32,16,2560]{2,1,0:T(8,128)(2,1)S(1)} %get-tuple-element.49.feats_ref, bf16[2560,2560]{1,0:T(8,128)(2,1)} %get-tuple-element.50.w_ref, bf16[32,16,2560]{2,1,0:T(8,128)(2,1)S(1)} %get-tuple-element.51.resid_ref, f32[4,2560]{1,0:T(4,128)S(1)} %get-tuple-element.52.gate_ref, ...), custom_call_target="tpu_custom_call" | custom-call | flops 7000000000 | bytes 30000000 | tf_op jit(solution)/shard_map/cond/branch_0_fun/pallas_call | solution.py:691
  215.8 2.4 %copy.19 = bf16[1,1,32,2,16,2560]{5,4,3,2,1,0:T(8,128)(2,1)} copy(bf16[1,1,32,2,16,2560]{5,4,3,2,1,0:T(8,128)(2,1)S(1)} %get-tuple-element.79) | data formatting | bytes 10485760
Async XLA Ops:
  1.6 95.2 %copy-start = (bf16[1,1,512,2560]{3,2,1,0:T(8,128)(2,1)S(1)}, bf16[1,1,512,2560]{3,2,1,0:T(8,128)(2,1)}, u32[]{:S(2)}) copy-start(bf16[1,1,512,2560]{3,2,1,0:T(8,128)(2,1)} %param.16) | copy-start | bytes 7864324
  1.6 95.2 %copy-start.1 = (f32[4,2560]{1,0:T(4,128)S(1)}, f32[4,2560]{1,0:T(4,128)}, u32[]{:S(2)}) copy-start(f32[4,2560]{1,0:T(4,128)} %param.18) | copy-start | bytes 122884
  1.6 95.2 %copy-start.2 = (f32[4]{0:T(128)S(1)}, f32[4]{0:T(128)}, u32[]{:S(2)}) copy-start(f32[4]{0:T(128)} %param.19) | copy-start | bytes 52
  1.6 95.2 %copy-start.3 = (s32[32]{0:T(128)S(1)}, s32[32]{0:T(128)}, u32[]{:S(2)}) copy-start(s32[32]{0:T(128)} %param.22) | copy-start | bytes 388

commit v3 on v1

v3 whole, which is shorter than its diff:
```python
import functools
import math

import jax
import jax.numpy as jnp
from jax import lax
from jax.experimental import pallas as pl
from jax.experimental.pallas import tpu as pltpu
from jax.sharding import PartitionSpec as P

MESH = pl.DeviceIdType.MESH
HS = 128
NX, NZ, NY = 4, 8, 4
NCLIP = 32
TOK = 512
NB = 32
BR = 16
HALF = 1280
HEADS = 10
INNER = 2560
WID = 2560
SHARD = 80
MAXH = 3
CAP = 4
CA = 1024
PART = {
    "A": ((0, CA), (0, CA // 2), (CA // 2, CA)),
    "B": ((CA, WID), (CA, (CA + WID) // 2), ((CA + WID) // 2, WID)),
}
CHUNKS = ((0, 512, "A"), (512, 1024, "A"), (1024, 1536, "B"), (1536, 2048, "B"), (2048, 2560, "B"))
PIECES = ((0, CA), (CA, WID))
ROWS = 256
ZRELS = (0, -1, 1, -2, 2, -3, 3, 4)
XRELS = (0, -1, 1, 2)


def plan():
    names = []
    for way in (1, -1):
        names += [("Bz", way, hop) for hop in (1, 2, 3, 4)]
        names += [("Ax", way, hop) for hop in (1, 2)]
        names += [("Az", way, hop, xrel) for hop in (1, 2, 3, 4) for xrel in XRELS]
        names += [("Bx", way, hop, zrel) for hop in (1, 2) for zrel in ZRELS]
    return {name: at for at, name in enumerate(names)}


NAMES = plan()
RING = {
    name: at
    for at, name in enumerate(
        [(way, hop, piece) for way in (1, -1) for hop in (1, 2, 3) for piece in (0, 1)] + [(1, 4, 0), (-1, 4, 1)]
    )
}


def remote(src, dst, send, recv, target):
    return pltpu.make_async_remote_copy(
        src_ref=src, dst_ref=dst, send_sem=send, recv_sem=recv, device_id=target, device_id_type=MESH
    )


def place():
    y = lax.axis_index("span")
    cl = lax.axis_index("clip")
    m = lax.axis_index("mp")
    return y, cl, m, cl // NZ, lax.rem(cl, NZ)


def tile_rows(r):
    return pl.ds(pl.multiple_of(r * ROWS, ROWS), ROWS)


def main_kernel(
    q_ref, k_ref, v_ref, resid_ref, w_ref, gate_ref, gain_ref, scale_ref, route_ref, len_ref, step_ref,
    out_ref, values_ref, table, most_ref,
    qkv, obuf, feats, wfull, resid, valbuf, sendbuf, ext, stage, sendx, tiles, ytiles, codes, table_s, codes_s,
    q_send, q_recv, o_send, o_recv, sib_send, sib_recv, w_send, w_recv, w_own, r_sem, v_sem,
    t_send, t_recv, t_here, y_send, y_recv, a_send, a_recv, e_send, e_recv, x_send, x_recv,
):
    y, cl, m, x, z = place()

    def clip_at(dx, dz):
        return lax.rem(x + (dx + NX), NX) * NZ + lax.rem(z + (dz + NZ), NZ)

    def first_head(yy):
        return (5 * yy + 1 - m) // 2

    def has_head(yy, i):
        return first_head(yy) + i < first_head(yy + 1)

    def cols128(at):
        return pl.ds(pl.multiple_of(at * HS, HS), HS)

    barrier = pltpu.get_barrier_semaphore()

    def greet(d, carry):
        pl.semaphore_signal(
            barrier, inc=1, device_id=(y, lax.rem(cl + d, NCLIP), m), device_id_type=MESH
        )
        return carry

    lax.fori_loop(1, NCLIP, greet, 0)
    for d in (1, 2, 3):
        pl.semaphore_signal(barrier, inc=1, device_id=(lax.rem(y + d, NY), cl, m), device_id_type=MESH)
    pl.semaphore_signal(barrier, inc=1, device_id=(y, cl, 1 - m), device_id_type=MESH)
    pl.semaphore_wait(barrier, NCLIP - 1 + 3 + 1)

    waited, sent = set(), []

    def rows_of(rel):
        return pl.ds(pl.multiple_of(clip_at(*rel) * SHARD, 16), SHARD)

    def w_start(name, rel, target, half=None, own=False):
        lo, hi = PART[name[0][0]][0 if half is None else 1 + half]
        dst = wfull.at[rows_of(rel), lo:hi]
        src = w_ref.at[:, lo:hi] if own else dst
        sent.append(hi - lo)
        remote(src, dst, w_send, w_recv.at[NAMES[name]], (y, clip_at(*target), m)).start()

    def w_wait(name, rel, half=None):
        if name in waited:
            return
        waited.add(name)
        lo, hi = PART[name[0][0]][0 if half is None else 1 + half]
        dst = wfull.at[rows_of(rel), lo:hi]
        remote(dst, dst, w_send, w_recv.at[NAMES[name]], (y, cl, m)).wait_recv()

    def half_of(way):
        return 0 if way == 1 else 1

    def bz_wait(way, hop):
        w_wait(("Bz", way, hop), (0, -way * hop), half_of(way) if hop == 4 else None)

    def ax_wait(way, hop):
        w_wait(("Ax", way, hop), (-way * hop, 0), half_of(way) if hop == 2 else None)

    def az_wait(way, hop, xrel):
        w_wait(("Az", way, hop, xrel), (xrel, -way * hop), half_of(way) if hop == 4 else None)

    def bx_wait(way, hop, zrel):
        w_wait(("Bx", way, hop, zrel), (-way * hop, zrel), half_of(way) if hop == 2 else None)

    def b_to_x(zrel, own=False):
        for way in (1, -1):
            w_start(("Bx", way, 1, zrel), (0, zrel), (way, 0), own=own)

    def a_to_z(xrel, own=False):
        for way in (1, -1):
            w_start(("Az", way, 1, xrel), (xrel, 0), (0, way), own=own)

    def bz_event(hop):
        for way in (1, -1):
            bz_wait(way, hop)
            if hop < 4:
                w_start(
                    ("Bz", way, hop + 1), (0, -way * hop), (0, way), half=half_of(way) if hop == 3 else None
                )
                b_to_x(-way * hop)
        if hop == 4:
            b_to_x(4)

    def ax_event(hop):
        for way in (1, -1):
            ax_wait(way, hop)
            if hop == 1:
                w_start(("Ax", way, 2), (-way, 0), (way, 0), half=half_of(way))
                a_to_z(-way)
        if hop == 2:
            a_to_z(2)

    def az_event(hop, xrel):
        for way in (1, -1):
            az_wait(way, hop, xrel)
            w_start(
                ("Az", way, hop + 1, xrel), (xrel, -way * hop), (0, way), half=half_of(way) if hop == 3 else None
            )

    def bx_event(zrel):
        for way in (1, -1):
            bx_wait(way, 1, zrel)
            w_start(("Bx", way, 2, zrel), (-way, zrel), (way, 0), half=half_of(way))

    def all_of(part):
        for way in (1, -1):
            if part == "A":
                for hop in (1, 2):
                    ax_wait(way, hop)
                for hop in (1, 2, 3, 4):
                    for xrel in XRELS:
                        az_wait(way, hop, xrel)
            else:
                for hop in (1, 2, 3, 4):
                    bz_wait(way, hop)
                for hop in (1, 2):
                    for zrel in ZRELS:
                        bx_wait(way, hop, zrel)

    tensors = (q_ref, k_ref, v_ref)

    def qkv_out(i, d):
        yy = lax.rem(y + d, NY)

        @pl.when(has_head(yy, i))
        def _():
            for t in range(3):
                remote(
                    tensors[t].at[:, cols128(first_head(yy) + i)],
                    qkv.at[i, y, t],
                    q_send.at[i, d],
                    q_recv.at[i, y],
                    (yy, cl, m),
                ).start()

    def qkv_here(i):
        @pl.when(has_head(y, i))
        def _():
            for t in range(3):
                pltpu.make_async_copy(
                    tensors[t].at[:, cols128(first_head(y) + i)], qkv.at[i, y, t], q_recv.at[i, y]
                ).start()

    def qkv_sent(i, d):
        yy = lax.rem(y + d, NY)

        @pl.when(has_head(yy, i))
        def _():
            remote(qkv.at[i, 0], qkv.at[i, 0], q_send.at[i, d], q_recv.at[i, 0], (yy, cl, m)).wait_send()

    def own_cols(head):
        return cols128(m * HEADS + head)

    def attend(i, c):
        @pl.when(has_head(y, i))
        def _():
            pltpu.make_async_copy(qkv.at[i, c], qkv.at[i, c], q_recv.at[i, c]).wait()

            def tile(r, carry):
                rows = tile_rows(r)
                query = qkv[i, c, 0, rows, :]
                to_two = 1.0 / (math.sqrt(HS) * math.log(2.0))
                ones = jnp.ones((TOK, HS), jnp.bfloat16)
                top = jnp.full((ROWS, 1), -jnp.inf, jnp.float32)
                acc = jnp.zeros((ROWS, 2 * HS), jnp.float32)
                for cc in range(c + 1):
                    scores = lax.dot_general(
                        query, qkv[i, cc, 1], (((1,), (1,)), ((), ())), preferred_element_type=jnp.float32
                    )
                    higher = jnp.maximum(top, jnp.max(scores, axis=1, keepdims=True))
                    prob = jnp.exp2((scores - higher) * to_two).astype(jnp.bfloat16)
                    val = jnp.concatenate([qkv[i, cc, 2], ones], axis=1)
                    acc = acc * jnp.exp2((top - higher) * to_two)
                    acc = acc + jnp.dot(prob, val, preferred_element_type=jnp.float32)
                    top = higher
                many = ROWS // BR
                done = (acc[:, :HS] / acc[:, HS:]).astype(jnp.bfloat16)
                obuf[i, c, pl.ds(r * many, many)] = done.reshape(many, BR, HS)
                return carry

            lax.fori_loop(0, TOK // ROWS, tile, 0, unroll=True)
            head = first_head(y) + i
            part = feats.at[:, :, own_cols(head)]

            @pl.when(y == c)
            def _():
                feats[:, :, own_cols(head)] = obuf[i, c]
                remote(obuf.at[i, c], part, sib_send, sib_recv, (y, cl, 1 - m)).start()

            @pl.when(y != c)
            def _():
                remote(obuf.at[i, c], part, o_send.at[i, c], o_recv.at[head], (c, cl, m)).start()

    def o_event(i):
        for d in (1, 3, 2):
            yy = lax.rem(y + d, NY)

            @pl.when(has_head(yy, i))
            def _(yy=yy):
                head = first_head(yy) + i
                part = feats.at[:, :, own_cols(head)]
                remote(part, part, o_send.at[i, 0], o_recv.at[head], (y, cl, m)).wait_recv()
                remote(part, part, sib_send, sib_recv, (y, cl, 1 - m)).start()

    def find_slots():
        shape = tiles.shape[1:]
        row_at = lax.broadcasted_iota(jnp.int32, shape, 0)
        group = lax.broadcasted_iota(jnp.int32, shape, 1)
        first = jnp.full(shape, NB, jnp.int32)
        second = jnp.full(shape, NB, jnp.int32)
        for b in range(NB):
            here = group == route_ref[b]
            second = jnp.where(here & (first < NB) & (second == NB), b, second)
            first = jnp.where(here & (first == NB), b, first)
        have = jnp.where(second < NB, 1, 0)
        upto = have
        for shift in (1, 2, 4, 8, 16):
            upto = upto + jnp.where(group >= shift, pltpu.roll(upto, shift, 1), 0)
        before = upto - have
        total = jnp.sum(have, axis=1, keepdims=True)
        code = jnp.where((have == 1) & (before < CAP), before, CAP)
        extra = jnp.zeros(shape, jnp.int32)
        for e in range(CAP):
            at = jnp.sum(jnp.where((have == 1) & (before == e), second, 0), axis=1, keepdims=True)
            extra = jnp.where(group == e, at, extra)
        table[...] = jnp.where(row_at == 0, first, jnp.where(row_at == 1, second, extra))
        tiles[cl] = jnp.where(row_at == 0, code, total)

        def tell(d, carry):
            g = lax.rem(cl + d, NCLIP)
            remote(tiles.at[cl], tiles.at[cl], t_send, t_recv, (y, g, m)).start()
            return carry

        lax.fori_loop(1, NCLIP, tell, 0)
        table_copy.start()

    def share_most():
        others = tiles.at[0 : NCLIP - 1]
        remote(others, others, t_send, t_recv, (y, cl, m)).wait_recv()
        codes[...] = tiles[:, 0, :]
        codes_copy.start()
        ytiles[y] = jnp.max(tiles[...], axis=0)
        for d in (1, 2, 3):
            remote(ytiles.at[y], ytiles.at[y], y_send.at[d], y_recv.at[y], (lax.rem(y + d, NY), cl, m)).start()

    def know_most():
        for d in (1, 2, 3):
            yy = lax.rem(y + d, NY)
            remote(ytiles.at[yy], ytiles.at[yy], y_send.at[d], y_recv.at[yy], (y, cl, m)).wait_recv()
        most_ref[...] = jnp.max(ytiles[...], axis=0)

    table_copy = pltpu.make_async_copy(table, table_s, t_here.at[0])
    codes_copy = pltpu.make_async_copy(codes, codes_s, t_here.at[1])

    w_start(("Bz", 1, 1), (0, 0), (0, 1), own=True)
    w_start(("Bz", -1, 1), (0, 0), (0, -1), own=True)
    for way in (1, -1):
        w_start(("Ax", way, 1), (0, 0), (way, 0), own=True)
    b_to_x(0, own=True)
    for i in range(MAXH):
        for d in (1, 3, 2):
            qkv_out(i, d)
        qkv_here(i)
        if i == 0:
            a_to_z(0, own=True)
    w_copy = pltpu.make_async_copy(w_ref, wfull.at[rows_of((0, 0)), :], w_own)
    w_copy.start()
    resid_copy = pltpu.make_async_copy(resid_ref, resid, r_sem)
    resid_copy.start()
    valbuf[NB] = jnp.zeros((BR, WID), jnp.bfloat16)
    stage[CAP] = jnp.zeros((BR, WID), jnp.bfloat16)

    events = [(1.0, find_slots), (24.0, share_most), (32.0, know_most)]
    for hop, at in ((1, 5.5), (2, 11.0), (3, 16.5), (4, 20.0)):
        events.append((at, functools.partial(bz_event, hop)))
    for hop, at in ((1, 4.0), (2, 7.0)):
        events.append((at, functools.partial(ax_event, hop)))
    for hop in (1, 2, 3):
        for n, xrel in enumerate(XRELS):
            events.append((17.0 + 13.0 * (hop - 1) + 3.3 * n, functools.partial(az_event, hop, xrel)))
    for n, zrel in enumerate(ZRELS):
        events.append((7.6 * (n + 1), functools.partial(bx_event, zrel)))
    for i, at, back in ((0, 17.0, 27.0), (1, 35.0, 45.0), (2, 50.0, 61.0)):
        for c in range(NY):
            events.append((at + 0.7 * c, functools.partial(attend, i, c)))
        events.append((back, functools.partial(o_event, i)))
    events.sort(key=lambda item: item[0])
    late = [act for at, act in events if at > 61.0]
    for at, act in events:
        if at <= 61.0:
            act()

    half_feats = feats.at[:, :, pl.ds(pl.multiple_of((1 - m) * HALF, HS), HALF)]
    remote(half_feats, half_feats, sib_send, sib_recv, (y, cl, 1 - m)).wait_recv()
    w_copy.wait()
    resid_copy.wait()
    table_copy.wait()
    codes_copy.wait()

    step, factor = step_and_factor(step_ref, len_ref, scale_ref, cl, y)

    def project(n):
        lo, hi, part = CHUNKS[n]
        all_of(part)
        many = ROWS // BR

        def tile(r, carry):
            blocks = pl.ds(r * many, many)
            feat = feats[blocks].reshape(ROWS, INNER)
            proj = jnp.dot(feat, wfull[:, lo:hi], preferred_element_type=jnp.float32)
            gate = gate_ref[pl.ds(step, 1), lo:hi]
            left = resid[blocks, :, lo:hi].reshape(ROWS, hi - lo).astype(jnp.float32)
            row = (left + gate * proj).astype(jnp.bfloat16)
            value = (row.astype(jnp.float32) * factor * gain_ref[lo:hi].reshape(1, hi - lo)).astype(jnp.bfloat16)
            valbuf[blocks, :, lo:hi] = value.reshape(many, BR, hi - lo)
            return carry

        lax.fori_loop(0, TOK // ROWS, tile, 0)

    def firsts(n):
        lo, hi, part = CHUNKS[n]

        def send(d, carry):
            g = lax.rem(cl + d, NCLIP)
            sendbuf[g, :, lo:hi] = valbuf[table_s[0, g], :, lo:hi]
            remote(
                sendbuf.at[g, :, lo:hi], out_ref.at[cl, 0, :, lo:hi], a_send.at[n], a_recv.at[n], (y, g, m)
            ).start()
            return carry

        lax.fori_loop(1, NCLIP, send, 0)
        sendbuf[cl, :, lo:hi] = valbuf[table_s[0, cl], :, lo:hi]
        pltpu.make_async_copy(sendbuf.at[cl, :, lo:hi], out_ref.at[cl, 0, :, lo:hi], a_recv.at[n]).start()

    def z_at(dz):
        return lax.rem(z + (dz + NZ), NZ)

    def ring_start(way, hop, piece):
        lo, hi = PIECES[piece]
        part = ext.at[z_at(-way * (hop - 1)), :, :, lo:hi]
        remote(part, part, e_send, e_recv.at[RING[way, hop, piece]], (y, clip_at(0, way), m)).start()

    def ring_wait(way, hop, piece):
        lo, hi = PIECES[piece]
        part = ext.at[z_at(-way * hop), :, :, lo:hi]
        remote(part, part, e_send, e_recv.at[RING[way, hop, piece]], (y, cl, m)).wait_recv()

    def seconds(piece):
        lo, hi = PIECES[piece]
        for e in range(CAP):
            ext[z, e, :, lo:hi] = valbuf[table_s[2, e], :, lo:hi]
        for way in (1, -1):
            ring_start(way, 1, piece)

    def ring_event(hop, piece):
        for way in (1, -1):
            if (way, hop, piece) in RING:
                ring_wait(way, hop, piece)
                if (way, hop + 1, piece) in RING:
                    ring_start(way, hop + 1, piece)

    def to_x(zrel):
        zs = z_at(zrel)
        source = x * NZ + zs
        stage[0:CAP] = ext[zs]
        for d in (1, 3, 2, 0):
            xx = lax.rem(x + d, NX)
            g = xx * NZ + z
            sendx[xx, zs] = stage[codes_s[source, g]]
            if d:
                remote(sendx.at[xx, zs], out_ref.at[source, 1], x_send, x_recv, (y, g, m)).start()
            else:
                pltpu.make_async_copy(sendx.at[xx, zs], out_ref.at[source, 1], x_recv).start()

    def next_late(many):
        for _ in range(many):
            if late:
                late.pop(0)()

    project(0)
    firsts(0)
    next_late(1)
    project(1)
    seconds(0)
    firsts(1)
    next_late(len(late))
    project(2)
    project(3)
    project(4)
    seconds(1)
    values_copy = pltpu.make_async_copy(valbuf.at[0:NB], values_ref, v_sem)
    values_copy.start()
    to_x(0)
    ring_event(1, 0)
    firsts(2)
    ring_event(1, 1)
    to_x(1)
    to_x(-1)
    ring_event(2, 0)
    firsts(3)
    ring_event(2, 1)
    to_x(2)
    to_x(-2)
    ring_event(3, 0)
    firsts(4)
    ring_event(3, 1)
    to_x(3)
    to_x(-3)
    ring_event(4, 0)
    ring_event(4, 1)
    to_x(4)

    assert len(waited) == len(NAMES) and sum(sent) == (NCLIP - 1) * WID and not late
    for n, (lo, hi, part) in enumerate(CHUNKS):
        most = sendbuf.at[0 : NCLIP - 1, :, lo:hi]
        remote(most, most, a_send.at[n], a_recv.at[n], (y, cl, m)).wait_send()
        whole = out_ref.at[:, 0, :, lo:hi]
        pltpu.make_async_copy(whole, whole, a_recv.at[n]).wait()
    most = ext.at[0 : NZ - 1]
    remote(most, most, e_send, e_recv.at[0], (y, cl, m)).wait_send()
    most = sendx.at[0 : NX - 1]
    remote(most, most, x_send, x_recv, (y, cl, m)).wait_send()
    whole = out_ref.at[:, 1]
    pltpu.make_async_copy(whole, whole, x_recv).wait()
    values_copy.wait()
    remote(half_feats, half_feats, sib_send, sib_recv, (y, cl, 1 - m)).wait_send()
    most = wfull.at[0 : (NCLIP - 1) * SHARD, :]
    remote(most, most, w_send, w_recv.at[0], (y, cl, m)).wait_send()
    others = tiles.at[0 : NCLIP - 1]
    remote(others, others, t_send, t_recv, (y, cl, m)).wait_send()
    for d in (1, 2, 3):
        remote(ytiles.at[0], ytiles.at[0], y_send.at[d], y_recv.at[0], (y, cl, m)).wait_send()
    for i in range(MAXH):
        for d in (1, 2, 3):
            qkv_sent(i, d)
        for c in range(NY):

            @pl.when(has_head(y, i) & (y != c))
            def _(i=i, c=c):
                remote(obuf.at[i, c], obuf.at[i, c], o_send.at[i, c], o_recv.at[0], (y, cl, m)).wait_send()


def step_and_factor(step_ref, len_ref, scale_ref, cl, y):
    step = step_ref[y, cl]
    live = jnp.where(y < len_ref[cl], 1.0, 0.0).astype(jnp.float32)
    return step, scale_ref[step] * live


def second_kernel(values_ref, table, out_ref, valbuf, sendbuf, v_sem, a_send, a_recv):
    y, cl, m, x, z = place()
    barrier = pltpu.get_barrier_semaphore()

    def greet(d, carry):
        pl.semaphore_signal(
            barrier, inc=1, device_id=(y, lax.rem(cl + d, NCLIP), m), device_id_type=MESH
        )
        return carry

    lax.fori_loop(1, NCLIP, greet, 0)
    load = pltpu.make_async_copy(values_ref, valbuf.at[0:NB], v_sem)
    load.start()
    load.wait()
    valbuf[NB] = jnp.zeros((BR, WID), jnp.bfloat16)
    pl.semaphore_wait(barrier, NCLIP - 1)

    def send(d, carry):
        g = lax.rem(cl + d, NCLIP)
        sendbuf[g] = valbuf[table[1, g]]
        remote(sendbuf.at[g], out_ref.at[cl], a_send, a_recv, (y, g, m)).start()
        return carry

    lax.fori_loop(1, NCLIP, send, 0)
    sendbuf[cl] = valbuf[table[1, cl]]
    pltpu.make_async_copy(sendbuf.at[cl], out_ref.at[cl], a_recv).start()
    most = sendbuf.at[0 : NCLIP - 1]
    remote(most, most, a_send, a_recv, (y, cl, m)).wait_send()
    pltpu.make_async_copy(out_ref, out_ref, a_recv).wait()


def shards(queries, keys, values, resid, out_weight, gate_table, step_scale, gain, route, clip_len, tstep):
    any_place = pl.BlockSpec(memory_space=pl.ANY)
    hbm = pl.BlockSpec(memory_space=pltpu.HBM)
    vmem = pl.BlockSpec(memory_space=pltpu.VMEM)
    smem = pl.BlockSpec(memory_space=pltpu.SMEM)
    dma = pltpu.SemaphoreType.DMA
    bf16, i32 = jnp.bfloat16, jnp.int32
    shape = jax.ShapeDtypeStruct
    scored, rows, table, most = pl.pallas_call(
        main_kernel,
        out_shape=(
            shape((NCLIP, 2, BR, WID), bf16),
            shape((NB, BR, WID), bf16),
            shape((8, 128), i32),
            shape((8, 128), i32),
        ),
        in_specs=[hbm] * 5 + [vmem] * 2 + [smem] * 4,
        out_specs=(any_place, hbm, vmem, vmem),
        scratch_shapes=[
            pltpu.VMEM((MAXH, NY, 3, TOK, HS), bf16),
            pltpu.VMEM((MAXH, NY, NB, BR, HS), bf16),
            pltpu.VMEM((NB, BR, INNER), bf16),
            pltpu.VMEM((INNER, WID), bf16),
            pltpu.VMEM((NB, BR, WID), bf16),
            pltpu.VMEM((NB + 1, BR, WID), bf16),
            pltpu.VMEM((NCLIP, BR, WID), bf16),
            pltpu.VMEM((NZ, CAP, BR, WID), bf16),
            pltpu.VMEM((CAP + 1, BR, WID), bf16),
            pltpu.VMEM((NX, NZ, BR, WID), bf16),
            pltpu.VMEM((NCLIP, 8, 128), i32),
            pltpu.VMEM((NY, 8, 128), i32),
            pltpu.VMEM((NCLIP, 128), i32),
            pltpu.SMEM((8, 128), i32),
            pltpu.SMEM((NCLIP, 128), i32),
            dma((MAXH, NY)),
            dma((MAXH, NY)),
            dma((MAXH, NY)),
            dma((HEADS,)),
            dma,
            dma,
            dma,
            dma((len(NAMES),)),
            dma,
            dma,
            dma,
            dma,
            dma,
            dma((2,)),
            dma((NY,)),
            dma((NY,)),
            dma((len(CHUNKS),)),
            dma((len(CHUNKS),)),
            dma,
            dma((len(RING),)),
            dma,
            dma,
        ],
        compiler_params=pltpu.CompilerParams(
            collective_id=0, has_side_effects=True, vmem_limit_bytes=58 * 1024 * 1024
        ),
        cost_estimate=pl.CostEstimate(flops=11_000_000_000, bytes_accessed=40_000_000, transcendentals=8_000_000),
    )(
        queries[0, 0],
        keys[0, 0],
        values[0, 0],
        resid[0, 0].reshape(NB, BR, WID),
        out_weight,
        gate_table,
        gain,
        step_scale,
        route[0, 0, :, 0],
        clip_len,
        tstep.T,
    )

    def direct(scored, rows, table):
        second = pl.pallas_call(
            second_kernel,
            out_shape=shape((NCLIP, BR, WID), bf16),
            in_specs=[hbm, smem],
            out_specs=hbm,
            scratch_shapes=[
                pltpu.VMEM((NB + 1, BR, WID), bf16),
                pltpu.VMEM((NCLIP, BR, WID), bf16),
                dma,
                dma,
                dma,
            ],
            compiler_params=pltpu.CompilerParams(
                collective_id=1, has_side_effects=True, vmem_limit_bytes=16 * 1024 * 1024
            ),
        )(rows, table)
        return jnp.concatenate([scored[:, :1], second[:, None]], axis=1)

    scored = lax.cond(most[1, 0] <= CAP, lambda scored, rows, table: scored, direct, scored, rows, table)
    return scored[None, None]


def solution(mesh):
    placed = (
        P("clip", "span", None, "mp"),
        P("clip", "span", None, "mp"),
        P("clip", "span", None, "mp"),
        P("clip", "span", None, "mp"),
        P("clip", "mp"),
        P(None, "mp"),
        P(),
        P("mp"),
        P("clip", "span", None, None),
        P(),
        P(),
    )
    return jax.shard_map(
        shards,
        mesh=mesh,
        in_specs=placed,
        out_specs=P("span", "clip", None, None, None, "mp"),
        check_vma=False,
    )
```

time: 212 us -> 182 us (0.86)
  Pallas kernels: 203 us -> 177 us
  local copies, waits for them, and re-layouts: 8.11 us -> 3.55 us
    pallas_call x1, Pallas kernels: 203 us -> 177 us  [shards(): pl.pallas_call(main_kernel, out_shape=(shape((NCLIP, 2, BR, WID), bf16),...]
    unnamed x2 -> x1, local copies, waits for them, and re-layouts: 6.15 us -> 2.36 us
where the time goes in v3:
time: 182 us; the launch traced here: 181 us
  Pallas kernels  177 us (97%)
  local copies, waits for them, and re-layouts  3.55 us (2%)
    pallas_call x1, Pallas kernels, shards(): pl.pallas_call(main_kernel, out_shape=(shape((NCLIP, 2, BR, WID), bf16),...  177 us

profile of v3, /device:TPU:25, one launch (start us, length us, event | category | flops | bytes accessed | tf_op | source)
XLA Modules:
  0.0 181.4 jit_solution(14580006587993992663)
XLA Ops:
  0.0 177.2 %shard_map.111 = (bf16[32,2,16,2560]{3,2,1,0:T(8,128)(2,1)S(1)}, bf16[32,16,2560]{2,1,0:T(8,128)(2,1)}, s32[8,128]{1,0:T(8,128)S(1)}, s32[8,128]{1,0:T(8,128)}) custom-call(bf16[512,1280]{1,0:T(8,128)(2,1)} %bitcast.14, bf16[512,1280]{1,0:T(8,128)(2,1)} %bitcast.15, bf16[512,1280]{1,0:T(8,128)(2,1)} %bitcast.16, bf16[32,16,2560]{2,1,0:T(8,128)(2,1)} %bitcast.13, ...), custom_call_target="tpu_custom_call" | custom-call | flops 11000000512 | bytes 40000000 | tf_op jit(solution)/shard_map/pallas_call | solution.py:566
  177.2 1.2 slice.6
  179.1 2.4 %copy.25 = bf16[1,1,32,2,16,2560]{5,4,3,2,1,0:T(8,128)(2,1)} copy(bf16[1,1,32,2,16,2560]{5,4,3,2,1,0:T(8,128)(2,1)S(1)} %get-tuple-element.32) | data formatting | bytes 10485760
  (1 shorter events, 0.0 us)

commit v4 on v3

--- a/solution.py
+++ b/solution.py
@@ -317,7 +317,7 @@
         remote(others, others, t_send, t_recv, (y, cl, m)).wait_recv()
         codes[...] = tiles[:, 0, :]
         codes_copy.start()
-        ytiles[y] = jnp.max(tiles[...], axis=0)
+        ytiles[y] = jnp.max(tiles[:, 1:2, :], axis=0) + jnp.zeros((8, 128), jnp.int32)
         for d in (1, 2, 3):
             remote(ytiles.at[y], ytiles.at[y], y_send.at[d], y_recv.at[y], (lax.rem(y + d, NY), cl, m)).start()
 
@@ -325,7 +325,7 @@
         for d in (1, 2, 3):
             yy = lax.rem(y + d, NY)
             remote(ytiles.at[yy], ytiles.at[yy], y_send.at[d], y_recv.at[yy], (y, cl, m)).wait_recv()
-        most_ref[...] = jnp.max(ytiles[...], axis=0)
+        most_ref[0, 0] = jnp.max(ytiles[...])
 
     table_copy = pltpu.make_async_copy(table, table_s, t_here.at[0])
     codes_copy = pltpu.make_async_copy(codes, codes_s, t_here.at[1])
@@ -569,10 +569,10 @@
             shape((NCLIP, 2, BR, WID), bf16),
             shape((NB, BR, WID), bf16),
             shape((8, 128), i32),
-            shape((8, 128), i32),
+            shape((1, 1), i32),
         ),
         in_specs=[hbm] * 5 + [vmem] * 2 + [smem] * 4,
-        out_specs=(any_place, hbm, vmem, vmem),
+        out_specs=(any_place, hbm, vmem, smem),
         scratch_shapes=[
             pltpu.VMEM((MAXH, NY, 3, TOK, HS), bf16),
             pltpu.VMEM((MAXH, NY, NB, BR, HS), bf16),
@@ -649,7 +649,7 @@
         )(rows, table)
         return jnp.concatenate([scored[:, :1], second[:, None]], axis=1)
 
-    scored = lax.cond(most[1, 0] <= CAP, lambda scored, rows, table: scored, direct, scored, rows, table)
+    scored = lax.cond(most[0, 0] <= CAP, lambda scored, rows, table: scored, direct, scored, rows, table)
     return scored[None, None]
 
 

time: 182 us -> 180 us (0.989)
  no operation moved by 1% of the time
where the time goes in v4:
time: 180 us
  Pallas kernels  177 us (98%)
  local copies, waits for them, and re-layouts  2.36 us (1%)
    pallas_call x1, Pallas kernels, shards(): pl.pallas_call(main_kernel, out_shape=(shape((NCLIP, 2, BR, WID), bf16),...  177 us

profile of v4, /device:TPU:25, one launch (start us, length us, event | category | flops | bytes accessed | tf_op | source)
XLA Modules:
  0.0 180.2 jit_solution(5766422427348694834)
XLA Ops:
  0.0 177.2 %shard_map.111 = (bf16[32,2,16,2560]{3,2,1,0:T(8,128)(2,1)S(1)}, bf16[32,16,2560]{2,1,0:T(8,128)(2,1)}, s32[8,128]{1,0:T(8,128)S(1)}, s32[1,1]{1,0:T(1,128)}) custom-call(bf16[512,1280]{1,0:T(8,128)(2,1)} %bitcast.14, bf16[512,1280]{1,0:T(8,128)(2,1)} %bitcast.15, bf16[512,1280]{1,0:T(8,128)(2,1)} %bitcast.16, bf16[32,16,2560]{2,1,0:T(8,128)(2,1)} %bitcast.13, ...), custom_call_target="tpu_custom_call" | custom-call | flops 11000000512 | bytes 40000000 | tf_op jit(solution)/shard_map/pallas_call | solution.py:566
  177.9 2.4 %copy.25 = bf16[1,1,32,2,16,2560]{5,4,3,2,1,0:T(8,128)(2,1)} copy(bf16[1,1,32,2,16,2560]{5,4,3,2,1,0:T(8,128)(2,1)S(1)} %get-tuple-element.32) | data formatting | bytes 10485760
  (1 shorter events, 0.0 us)
